TPU v7x, 128 devices: a whole 4x4x4 slice. The times are simulated.
128 devices in a mesh: dp: 32 (over x, y, core), rep: 4 (over z).
Axes of the slice: x: 4, y: 4, z: 4, core: 2. Of those that a mesh axis runs over, the one named last changes fastest.
Arguments:
- clip_tiles: bfloat16 [16384, 256, 128], P(('dp', 'rep')), may hold values from -16 to 16
- clip_size: int32 [128, 64], P(('dp', 'rep')), may hold values from 0 to 8, as said below
- clip_dest: int32 [128, 64], P(('dp', 'rep')), may hold values from 0 to 31, as said below
- timesteps: int32 [128, 64], P(('dp', 'rep')), may hold values from 0 to 999
- noise_seeds: int32 [128, 64], P(('dp', 'rep')), may hold values from 0 to 1048575
- w_time: bfloat16 [256, 256], replicated, may hold values from -0.375 to 0.375
- gain: float32 [128], replicated, may hold values from 0.1 to 1.9
- w_in: bfloat16 [128, 256], replicated, may hold values from -0.5 to 0.5
- w_out: bfloat16 [256, 128], replicated, may hold values from -0.375 to 0.375
- w_down: bfloat16 [512, 256], replicated, may hold values from -0.25 to 0.25
- w_up: bfloat16 [256, 512], replicated, may hold values from -0.375 to 0.375
Outputs:
- grad_time: float32 [256, 256], replicated
- grad_gain: float32 [128], replicated
- grad_in: float32 [128, 256], replicated
- grad_out: float32 [256, 128], replicated
- grad_down: float32 [512, 256], replicated
- grad_up: float32 [256, 512], replicated
- device_loss: float32 [128], P(('dp', 'rep'))
Inputs may be any that keep to these rules, and one draw needn't show every extreme that they name: `clip_size`: each loader's entries come in runs of four (entries 4j to 4j+3) that together hold exactly 8 tiles or none, the holding runs first; sizes are 0, 1, 2, 4 or 8. In every replica group the loaders hold 256 such runs in all, one loader holds 16 and one none. `clip_dest`: all entries of one run of four share one destination. Within a replica group every compute device receives exactly 64 tiles, and one loader sends at most 8 tiles to one compute device, some loader exactly 8.
All inputs are finite; a program needn't handle non-finite values.
Results may differ from a plain program's by a relative error of at most 0.00034.
Values may be sent and summed in bfloat16 or wider, within the bound.
A program may use at most 128 MiB of HBM per device.

v0:
```python
import math

import jax
import jax.numpy as jnp
from jax import lax
from jax.sharding import PartitionSpec as P

EMB = 256
GN_GROUPS = 32
TR = 8
TC = 32
TSTEPS = 1000


def hashed_noise(seed_grid, position):
    mixed = position * 1103515245 + seed_grid * 747796405 + 1013904223
    mixed = mixed ^ mixed >> 16 & 65535
    mixed = mixed * 73244475
    mixed = mixed ^ mixed >> 16 & 65535
    mixed = mixed * 73244475
    mixed = mixed ^ mixed >> 16 & 65535
    uniform_bits = mixed >> 8 & 16777215
    unit_value = (uniform_bits.astype(jnp.float32) + 0.5) * (1.0 / 16777216.0)
    return 1.7320508 * (2.0 * unit_value - 1.0)


def silu_slope(value):
    sigma = jax.nn.sigmoid(value)
    return sigma * (1.0 + value * (1.0 - sigma))


def to_patches(field):
    tile_count, pixel_count, channels = field.shape
    grid = field.reshape(tile_count, TR // 2, 2, TC // 2, 2, channels)
    return grid.transpose(0, 1, 3, 2, 4, 5).reshape(tile_count, pixel_count // 4, 4 * channels)


def from_patches(patch_field):
    tile_count, quarter, wide_count = patch_field.shape
    channels = wide_count // 4
    grid = patch_field.reshape(tile_count, TR // 2, TC // 2, 2, 2, channels)
    return grid.transpose(0, 1, 3, 2, 4, 5).reshape(tile_count, quarter * 4, channels)


def tile_meta(sizes_row, dest_row, time_row, seed_row, tile_count):
    clip_count = sizes_row.shape[0]
    ends = jnp.cumsum(sizes_row, dtype=jnp.int32)
    starts = ends - sizes_row
    tile_index = jnp.arange(tile_count, dtype=jnp.int32)
    owner = jnp.sum(
        (ends[None, :] <= tile_index[:, None]).astype(jnp.int32), axis=1, dtype=jnp.int32
    )
    onehot = (owner[:, None] == jnp.arange(clip_count, dtype=jnp.int32)[None, :]).astype(jnp.int32)

    def lookup(values):
        return jnp.sum(onehot * values[None, :], axis=1, dtype=jnp.int32)

    usable = (owner < clip_count).astype(jnp.int32)
    within = (tile_index - lookup(starts)) * usable
    tile_info = jnp.stack(
        [usable, within, lookup(sizes_row), lookup(time_row), lookup(seed_row)], axis=1
    )
    return (tile_info, lookup(dest_row))


def process(tile_data, tile_info, w_time, gain, w_in, w_out, w_down, w_up, loaders):
    highest = lax.Precision.HIGHEST
    row_count, pixel_count, channels = tile_data.shape
    usable = tile_info[:, 0] > 0
    within = tile_info[:, 1]
    clip_len = jnp.where(usable, tile_info[:, 2], 1)
    step_float = tile_info[:, 3].astype(jnp.float32)
    seed_grid = tile_info[:, 4][:, None, None]
    position = (
        within[:, None, None] * pixel_count
        + jnp.arange(pixel_count, dtype=jnp.int32)[None, :, None]
    ) * channels + jnp.arange(channels, dtype=jnp.int32)[None, None, :]
    noise_field = hashed_noise(seed_grid, position)
    alpha_bar = jnp.cos(((step_float + 1.0) / TSTEPS + 0.008) / 1.008 * (math.pi / 2.0)) ** 2
    noisy = (
        jnp.sqrt(alpha_bar)[:, None, None] * tile_data.astype(jnp.float32)
        + jnp.sqrt(1.0 - alpha_bar)[:, None, None] * noise_field
    )
    group_width = channels // GN_GROUPS
    grouped = noisy.reshape(row_count, pixel_count, GN_GROUPS, group_width)
    first_sum = jnp.sum(grouped, axis=(1, 3))
    square_sum = jnp.sum(grouped * grouped, axis=(1, 3))
    opening = (usable & (within == 0)).astype(jnp.int32)
    segment = jnp.cumsum(opening, dtype=jnp.int32) - 1
    member = (
        (segment[:, None] == jnp.arange(row_count, dtype=jnp.int32)[None, :]) & usable[:, None]
    ).astype(jnp.float32)
    clip_first = jnp.dot(member.T, first_sum, precision=highest)
    clip_square = jnp.dot(member.T, square_sum, precision=highest)
    tile_first = jnp.dot(member, clip_first, precision=highest)
    tile_square = jnp.dot(member, clip_square, precision=highest)
    denominator = (clip_len * (pixel_count * group_width)).astype(jnp.float32)[:, None]
    group_mean = tile_first / denominator
    variance = tile_square / denominator - group_mean * group_mean
    inv_spread = lax.rsqrt(variance + 1e-05)
    loss_weight = jnp.where(
        usable, 2.0 / (clip_len.astype(jnp.float32) * pixel_count * loaders), 0.0
    )
    mean_weight = jnp.where(
        usable, 1.0 / (clip_len.astype(jnp.float32) * (pixel_count * channels)), 0.0
    )
    half_width = EMB // 2
    frequency = jnp.exp(-math.log(10000.0) * jnp.arange(half_width, dtype=jnp.float32) / half_width)
    angle = step_float[:, None] * frequency[None, :]
    embedding = jnp.concatenate([jnp.cos(angle), jnp.sin(angle)], axis=1).astype(jnp.bfloat16)
    modulation = jnp.dot(embedding, w_time, preferred_element_type=jnp.float32)
    block_tiles = math.gcd(row_count, 16)

    def one_block(block_index, totals):
        start = block_index * block_tiles

        def take_block(values):
            return lax.dynamic_slice_in_dim(values, start, block_tiles, 0)

        noisy_block = take_block(noisy)
        noise_block = take_block(noise_field)
        mean_block = take_block(group_mean)
        spread_block = take_block(inv_spread)
        weight_block = take_block(loss_weight)
        mean_weight_block = take_block(mean_weight)
        embed_block = take_block(embedding)
        modul_block = take_block(modulation)
        group_view = noisy_block.reshape(block_tiles, pixel_count, GN_GROUPS, group_width)
        normed = (
            (group_view - mean_block[:, None, :, None]) * spread_block[:, None, :, None]
        ).reshape(block_tiles, pixel_count, channels)
        film_scale = modul_block[:, None, :channels]
        film_shift = modul_block[:, None, channels:]
        normal_in = (normed * gain * (1.0 + film_scale) + film_shift).astype(jnp.bfloat16)
        pre_hidden = jnp.einsum("rpc,ch->rph", normal_in, w_in, preferred_element_type=jnp.float32)
        hidden = jax.nn.silu(pre_hidden).astype(jnp.bfloat16)
        residual_out = noisy_block + jnp.einsum(
            "rph,hc->rpc", hidden, w_out, preferred_element_type=jnp.float32
        )
        patches = to_patches(residual_out.astype(jnp.bfloat16))
        pre_down = jnp.einsum("rqk,kd->rqd", patches, w_down, preferred_element_type=jnp.float32)
        down_act = jax.nn.silu(pre_down).astype(jnp.bfloat16)
        lifted = jnp.einsum("rqd,dk->rqk", down_act, w_up, preferred_element_type=jnp.float32)
        prediction = residual_out + from_patches(lifted)
        error = prediction - noise_block
        tile_loss = jnp.sum(error * error, axis=(1, 2)) * mean_weight_block
        grad_pred = error * weight_block[:, None, None]
        grad_lifted = to_patches(grad_pred).astype(jnp.bfloat16)
        add_up = jnp.einsum(
            "rqd,rqk->dk", down_act, grad_lifted, preferred_element_type=jnp.float32
        )
        grad_pre_down = (
            jnp.einsum("rqk,dk->rqd", grad_lifted, w_up, preferred_element_type=jnp.float32)
            * silu_slope(pre_down)
        ).astype(jnp.bfloat16)
        add_down = jnp.einsum(
            "rqk,rqd->kd", patches, grad_pre_down, preferred_element_type=jnp.float32
        )
        back_patch = jnp.einsum(
            "rqd,kd->rqk", grad_pre_down, w_down, preferred_element_type=jnp.float32
        )
        grad_residual = (grad_pred + from_patches(back_patch)).astype(jnp.bfloat16)
        add_out = jnp.einsum(
            "rph,rpc->hc", hidden, grad_residual, preferred_element_type=jnp.float32
        )
        grad_pre_hidden = (
            jnp.einsum("rpc,hc->rph", grad_residual, w_out, preferred_element_type=jnp.float32)
            * silu_slope(pre_hidden)
        ).astype(jnp.bfloat16)
        add_in = jnp.einsum(
            "rpc,rph->ch", normal_in, grad_pre_hidden, preferred_element_type=jnp.float32
        )
        grad_normal = jnp.einsum(
            "rph,ch->rpc", grad_pre_hidden, w_in, preferred_element_type=jnp.float32
        )
        add_gain = jnp.sum(grad_normal * normed * (1.0 + film_scale), axis=(0, 1))
        grad_scale = jnp.sum(grad_normal * normed * gain, axis=1)
        grad_shift = jnp.sum(grad_normal, axis=1)
        grad_modul = jnp.concatenate([grad_scale, grad_shift], axis=1)
        add_time = jnp.einsum(
            "re,rf->ef", embed_block.astype(jnp.float32), grad_modul, precision=highest
        )
        losses = lax.dynamic_update_slice_in_dim(totals[6], tile_loss, start, 0)
        return (
            totals[0] + add_time,
            totals[1] + add_gain,
            totals[2] + add_in,
            totals[3] + add_out,
            totals[4] + add_down,
            totals[5] + add_up,
            losses,
        )

    zeros = (
        jnp.zeros(w_time.shape, jnp.float32),
        jnp.zeros(gain.shape, jnp.float32),
        jnp.zeros(w_in.shape, jnp.float32),
        jnp.zeros(w_out.shape, jnp.float32),
        jnp.zeros(w_down.shape, jnp.float32),
        jnp.zeros(w_up.shape, jnp.float32),
        jnp.zeros((row_count,), jnp.float32),
    )
    return lax.fori_loop(0, row_count // block_tiles, one_block, zeros)


def body(
    clip_tiles,
    clip_size,
    clip_dest,
    timesteps,
    noise_seeds,
    w_time,
    gain,
    w_in,
    w_out,
    w_down,
    w_up,
):
    loaders = lax.axis_size("dp") * lax.axis_size("rep")
    dp_count = lax.axis_size("dp")
    tile_count = clip_tiles.shape[0]
    tile_info, dest_tile = tile_meta(
        clip_size[0], clip_dest[0], timesteps[0], noise_seeds[0], tile_count
    )
    spans = tile_count // 8
    capacity = 8 * ((spans + dp_count - 1) // dp_count)
    slot_total = dp_count * capacity
    usable = tile_info[:, 0]
    pick_dest = (dest_tile[:, None] == jnp.arange(dp_count, dtype=jnp.int32)[None, :]).astype(
        jnp.int32
    ) * usable[:, None]
    earlier = jnp.cumsum(pick_dest, axis=0, dtype=jnp.int32) - pick_dest
    slot_within = jnp.sum(earlier * pick_dest, axis=1, dtype=jnp.int32)
    target = jnp.where(usable > 0, dest_tile * capacity + slot_within, slot_total)
    outgoing = (
        jnp.zeros((slot_total,) + clip_tiles.shape[1:], clip_tiles.dtype)
        .at[target]
        .set(clip_tiles, mode="drop")
    )
    outgoing_info = jnp.zeros((slot_total, 5), jnp.int32).at[target].set(tile_info, mode="drop")
    arrived, arrived_info = (
        lax.all_to_all(outgoing, "dp", split_axis=0, concat_axis=0, tiled=True),
        lax.all_to_all(outgoing_info, "dp", split_axis=0, concat_axis=0, tiled=True),
    )
    received_count = tile_count // 2
    present = arrived_info[:, 0]
    ranking = jnp.cumsum(present, dtype=jnp.int32) - 1
    gather_index = (
        jnp.zeros((received_count,), jnp.int32)
        .at[jnp.where(present > 0, ranking, received_count)]
        .set(jnp.arange(slot_total, dtype=jnp.int32), mode="drop")
    )
    work_tiles = arrived[gather_index]
    work_info = arrived_info[gather_index]
    partial_grads = process(work_tiles, work_info, w_time, gain, w_in, w_out, w_down, w_up, loaders)
    own_loss = jnp.sum(partial_grads[6]).reshape(1)
    summed = lax.psum(
        (
            partial_grads[0],
            partial_grads[1],
            partial_grads[2],
            partial_grads[3],
            partial_grads[4],
            partial_grads[5],
        ),
        ("dp", "rep"),
    )
    return (summed[0], summed[1], summed[2], summed[3], summed[4], summed[5], own_loss)


def solution(mesh):
    in_specs = (
        P(("dp", "rep"), None, None),
        P(("dp", "rep"), None),
        P(("dp", "rep"), None),
        P(("dp", "rep"), None),
        P(("dp", "rep"), None),
        P(),
        P(),
        P(),
        P(),
        P(),
        P(),
    )
    out_specs = (P(), P(), P(), P(), P(), P(), P(("dp", "rep")))
    return jax.shard_map(body, mesh=mesh, in_specs=in_specs, out_specs=out_specs, check_vma=False)
```

profile of v0, /device:TPU:1, one launch (start us, length us, event | category | flops | bytes accessed | tf_op | source)
XLA Modules:
  0.0 721.3 jit_solution(11544506018478872541)
XLA Ops:
  11.9 8.6 %all-to-all-start = ((s32[32,8,5]{2,1,0:T(8,128)}), s32[32,8,5]{2,1,0:T(8,128)S(1)}, u32[]{:S(2)}, u32[]{:S(2)}) async-start(s32[32,8,5]{2,1,0:T(8,128)} %bitcast.13), calls=%async_computation | async-start | bytes 262144 | tf_op jit(solution)/shard_map/all_to_all | solution.py:243
  20.5 6.3 broadcast_in_dim.94
  26.7 21.7 %scatter_fusion = bf16[256,256,128]{2,1,0:T(8,128)(2,1)} fusion(bf16[256,256,128]{2,1,0:T(8,128)(2,1)} %broadcast_in_dim.94, s32[128]{0:T(128)S(1)} %get-tuple-element.526, bf16[128,256,128]{2,1,0:T(8,128)(2,1)} %param.13), kind=kCustom, calls=%fused_computation.4 | custom fusion | bytes 25166336 | tf_op jit(solution)/shard_map/scatter | solution.py:238
  48.4 9.0 %all-to-all-start.1 = ((bf16[256,256,128]{2,1,0:T(8,128)(2,1)}), bf16[256,256,128]{2,1,0:T(8,128)(2,1)}, u32[]{:S(2)}, u32[]{:S(2)}) async-start(bf16[256,256,128]{2,1,0:T(8,128)(2,1)} %scatter_fusion), calls=%async_computation.1 | async-start | bytes 33554432 | tf_op jit(solution)/shard_map/all_to_all | solution.py:242
  63.8 224.8 %all-to-all-done.1 = bf16[256,256,128]{2,1,0:T(8,128)(2,1)} async-done(((bf16[256,256,128]{2,1,0:T(8,128)(2,1)}), bf16[256,256,128]{2,1,0:T(8,128)(2,1)}, u32[]{:S(2)}, u32[]{:S(2)}) %all-to-all-start.1) | async-done | bytes 16777248 | tf_op jit(solution)/shard_map/all_to_all | solution.py:242
  288.6 8.8 %gather_fusion.1 = bf16[64,256,128]{2,1,0:T(8,128)(2,1)} fusion(bf16[256,256,128]{2,1,0:T(8,128)(2,1)} %all-to-all-done.1, s32[1024]{0:T(1024)S(1)} %pad_clamp_fusion), kind=kCustom, calls=%fused_computation.1 | custom fusion | bytes 8388864 | tf_op jit(solution)/shard_map/gather | solution.py:253
  297.4 14.6 %multiply_add_fusion = (f32[64,256,128]{2,1,0:T(8,128)S(1)}, f32[64,256,128]{2,1,0:T(8,128)}, f32[64,256,128]{2,1,0:T(8,128)}) fusion(bf16[64,256,128]{2,1,0:T(8,128)(2,1)} %gather_fusion.1, s32[128]{0:T(128)S(1)} %add.369, f32[64]{0:T(128)S(1)} %multiply_bitcast_fusion, s32[64]{0:T(128)S(1)} %get-tuple-element.447, s32[64,256]{1,0:T(8,128)S(1)} %add_multiply_fusion, ...), kind=kLoop, calls=%fused_computation.57 | loop fusion | flops 102760448 | bytes 29426944 | tf_op jit(solution)/shard_map/add | solution.py:81
  312.1 3.1 multiply_reduce_fusion.3
  316.9 199.4 %while.26 = (s32[]{:T(128)}, f32[256,256]{1,0:T(8,128)}, f32[128]{0:T(128)}, f32[128,256]{1,0:T(8,128)}, f32[256,128]{1,0:T(8,128)}, /*index=5*/f32[512,256]{1,0...) while((s32[]{:T(128)}, f32[256,256]{1,0:T(8,128)}, ...), condition=%wide.region_24.25_spmd.clone, body=%wide.region_19.24_spmd.clone.sunk | while | flops 3270510848 | bytes 184988272 | solution.py:203
  318.6 4.8 multiply_convert_fusion.13
  324.7 3.7 fusion.128
  333.1 2.6 reshape.403
  344.4 3.0 fusion.137
  352.1 3.5 reshape.404
  355.6 2.7 copy.93
  368.3 4.8 multiply_convert_fusion.13
  374.4 3.7 fusion.128
  394.1 3.1 fusion.137
  401.9 3.5 reshape.404
  405.5 2.7 copy.93
  418.2 4.8 multiply_convert_fusion.13
  424.3 3.7 fusion.128
  443.9 3.1 fusion.137
  451.8 3.5 reshape.404
  455.3 2.7 copy.93
  468.0 4.8 multiply_convert_fusion.13
  474.1 3.7 fusion.128
  493.7 3.1 fusion.137
  501.6 3.5 reshape.404
  505.1 2.7 copy.93
  517.6 103.2 %psum.43 = f32[128]{0:T(128)} all-reduce(f32[128]{0:T(128)} %get-tuple-element.849), channel_id=1, replica_groups=mesh['dp'=32,'rep'=4] {'dp','rep'}, use_global_device_ids=true, to_apply=%region_26.27 | all-reduce | flops 128 | bytes 1024 | tf_op jit(solution)/shard_map/psum | solution.py:257
  620.8 85.1 %all-reduce.3.cloned.1.call-done = (f32[256,256]{1,0:T(8,128)}, f32[128,256]{1,0:T(8,128)}, f32[256,128]{1,0:T(8,128)}, f32[512,256]{1,0:T(8,128)}, f32[256,512]{1,0:T(8,128)}) async-done(((f32[256,256]{1,0:T(8,128)}, f32[128,256]{1,0:T(8,128)}, f32[256,128]{1,0:T(8,128)}, f32[512,256]{1,0:T(8,128)}, f32[256,512]{1,0:T(8,128)}), (f32[256,256]{1,0:T(8,128)}, f32[128,256]{1,0:T(8,128)}, f32[256,128]{1,0:T(8,128)}, ...) | async-done | bytes 1572880 | tf_op jit(solution)/shard_map/psum | solution.py:257
  (461 shorter events, 146.1 us)
Async XLA Ops:
  7.2 55.9 %copy-start = (bf16[256,256]{1,0:T(8,128)(2,1)S(1)}, bf16[256,256]{1,0:T(8,128)(2,1)}, u32[]{:S(2)}) copy-start(bf16[256,256]{1,0:T(8,128)(2,1)} %param.18) | copy-start | bytes 393220
  11.9 36.6 %all-to-all-start = ((s32[32,8,5]{2,1,0:T(8,128)}), s32[32,8,5]{2,1,0:T(8,128)S(1)}, u32[]{:S(2)}, u32[]{:S(2)}) async-start(s32[32,8,5]{2,1,0:T(8,128)} %bitcast.13), calls=%async_computation | async-start | bytes 262144 | tf_op jit(solution)/shard_map/all_to_all | solution.py:243
  48.4 240.2 %all-to-all-start.1 = ((bf16[256,256,128]{2,1,0:T(8,128)(2,1)}), bf16[256,256,128]{2,1,0:T(8,128)(2,1)}, u32[]{:S(2)}, u32[]{:S(2)}) async-start(bf16[256,256,128]{2,1,0:T(8,128)(2,1)} %scatter_fusion), calls=%async_computation.1 | async-start | bytes 33554432 | tf_op jit(solution)/shard_map/all_to_all | solution.py:242
  57.4 648.5 %all-reduce.3.cloned.1.call-start = ((), (), s32[]{:S(2)}) async-start(), calls=%async_computation.2 | async-start | bytes 3145728 | tf_op jit(solution)/shard_map/psum | solution.py:257
  312.0 4.9 copy-start.8
  312.0 4.9 copy-start.13
  312.0 4.9 copy-start.29
  312.1 4.9 copy-start.31
  312.1 4.9 copy-start.33
  317.8 5.6 copy-start.18
  317.9 5.5 copy-start.20
  355.6 3.1 copy-start.11
  358.7 3.6 slice-start
  367.5 5.6 copy-start.18
  367.6 5.5 copy-start.20
  394.1 3.1 copy-start.6
  394.1 3.1 copy-start.7
  405.5 3.1 copy-start.11
  408.6 3.6 slice-start
  417.3 5.6 copy-start.18
  417.4 5.5 copy-start.20
  443.9 3.1 copy-start.6
  443.9 3.1 copy-start.7
  455.3 3.1 copy-start.11
  458.4 3.6 slice-start
  467.2 5.6 copy-start.18
  467.3 5.5 copy-start.20
  493.7 3.1 copy-start.6
  493.7 3.1 copy-start.7
  505.1 3.1 copy-start.11
  508.2 3.6 slice-start
  516.3 198.2 %copy-start.1 = (bf16[256,256]{1,0:T(8,128)(2,1)S(1)}, bf16[256,256]{1,0:T(8,128)(2,1)}, u32[]{:S(2)}) copy-start(bf16[256,256]{1,0:T(8,128)(2,1)} %param.18) | copy-start | bytes 393220
  (110 other events, 214.6 us)
Sparse Core Ops, SparseCore 0:
  516.5 189.4 all-reduce.2
where the time goes:
time: 724 us; the launch traced here: 721 us
  waiting for transfers between devices  310 us (43%)
  local copies, waits for them, and re-layouts  140 us (19%)
  blocking collectives  103 us (14%)
  matrix products  93.7 us (13%)
  other arithmetic  40.5 us (6%)
  starting transfers between devices  17.6 us (2%)
  between operations  14.4 us (2%)
    all_to_all x1, waiting for transfers between devices, body(): lax.all_to_all(outgoing, 'dp', split_axis=0, concat_axis=0, tiled=True)  225 us
    psum x1, blocking collectives, body(): lax.psum((partial_grads[0], partial_grads[1], partial_grads[2], partial_g...  103 us
    psum x1, waiting for transfers between devices, body(): lax.psum((partial_grads[0], partial_grads[1], partial_grads[2], partial_g...  85.1 us
    reshape x16, local copies, waits for them, and re-layouts, from_patches(): grid = patch_field.reshape(tile_count, TR // 2, TC // 2, 2, 2, channels)  39.1 us
    while x264, local copies, waits for them, and re-layouts  26.9 us
    scatter x1, local copies, waits for them, and re-layouts, body(): outgoing = jnp.zeros((slot_total,) + clip_tiles.shape[1:], clip_tiles.dty...  21.7 us
    dot_general x4, matrix products, one_block(): jnp.einsum('rpc,ch->rph', normal_in, w_in, preferred_element_type=jnp.flo...  19.1 us
    convert_element_type x8, local copies, waits for them, and re-layouts, one_block(): grad_lifted = to_patches(grad_pred).astype(jnp.bfloat16)  16.7 us
  transfers between devices with their start and end apart: 3, of which 2 were waited for; matrix products, arithmetic and copies ran while one was open for 5% of the time, Pallas kernels for 0%

commit v1 on v0

v1 whole, which is shorter than its diff:
```python
import math

import jax
import jax.numpy as jnp
import numpy as np
from jax import lax
from jax.experimental import pallas as pl
from jax.experimental.pallas import tpu as pltpu
from jax.sharding import PartitionSpec as P

EMB = 256
TR = 8
TC = 32
TSTEPS = 1000
C = 128
PIX = 256
HID = 256
SPAN = 8
MUL_POS = 1103515245
MUL_SEED = 747796405
ADD_POS = 1013904223
MUL_MIX = 73244475
ROOT3 = 1.7320508
NOISE_A = float(np.float32(2.0 * ROOT3 / 16777216.0))
NOISE_B = float(np.float32(ROOT3 * (1.0 / 16777216.0 - 1.0)))
F32 = jnp.float32
BF16 = jnp.bfloat16


def wrap32(value):
    value &= 0xFFFFFFFF
    return value - (1 << 32) if value >= (1 << 31) else value


def dot(a, b):
    return lax.dot_general(a, b, (((1,), (0,)), ((), ())), preferred_element_type=F32)


def dot_bt(a, b):
    return lax.dot_general(a, b, (((1,), (1,)), ((), ())), preferred_element_type=F32)


def dot_at(a, b):
    return lax.dot_general(a, b, (((0,), (0,)), ((), ())), preferred_element_type=F32)


def shift_right(value, amount):
    return lax.shift_right_logical(value, jnp.int32(amount))


def group_sum(x, lane):
    pair = x + jnp.where(lane % 2 == 0, pltpu.roll(x, 127, 1), pltpu.roll(x, 1, 1))
    return pair + jnp.where(lane % 4 < 2, pltpu.roll(pair, 126, 1), pltpu.roll(pair, 2, 1))


def span_kernel(
    count_ref, mix_ref, sa_ref, sb_ref, weight_ref, seg_ref,
    tiles_hbm, col_ref, emb_ref, slot_ref, wt_ref, gain_ref,
    win_ref, wout_ref, wdown_ref, wup_ref,
    gt_ref, misc_ref, gin_ref, gout_ref, gdown_ref, gup_ref,
    buf, sem, itab, perm, modul, noise, noisy, x_s, hid, slope, resid, patch,
    dact, dslope, glift, gpd_s, gres, gph_s, s1_s, s2_s, loss_s, stat,
    win_h, wout_h, wdown_h, wup_h,
):
    count = count_ref[0]

    def fetch(span, slot):
        return pltpu.make_async_copy(
            tiles_hbm.at[pl.ds(span * SPAN, SPAN)], buf.at[slot], sem.at[slot]
        )

    @pl.when(count > 0)
    def _():
        fetch(0, 0).start()

    row = lax.broadcasted_iota(jnp.int32, (PIX, C), 0)
    lane = lax.broadcasted_iota(jnp.int32, (PIX, C), 1)
    quad, rest = row // 64, row % 64
    pixel = (2 * (rest // 16) + quad // 2) * TC + 2 * (rest % 16) + quad % 2
    itab[...] = (pixel * C + lane) * jnp.int32(MUL_POS)
    prow = lax.broadcasted_iota(jnp.int32, (PIX, PIX), 0)
    pcol = lax.broadcasted_iota(jnp.int32, (PIX, PIX), 1)
    pquad, prest = prow // 64, prow % 64
    ppix = (2 * (prest // 16) + pquad // 2) * TC + 2 * (prest % 16) + pquad % 2
    perm[...] = jnp.where(ppix == pcol, 1.0, 0.0).astype(BF16)
    modul[...] = dot(emb_ref[...], wt_ref[...])
    win_h[...] = win_ref[...] * jnp.asarray(0.5, BF16)
    wdown_h[...] = wdown_ref[...] * jnp.asarray(0.5, BF16)
    wout_h[...] = wout_ref[...] * jnp.asarray(0.5, BF16)
    wup_h[...] = wup_ref[...] * jnp.asarray(0.5, BF16)
    for ref in (gin_ref, gout_ref, gdown_ref, gup_ref, s1_s, s2_s, loss_s):
        ref[...] = jnp.zeros_like(ref)
    lane8 = lax.broadcasted_iota(jnp.int32, (SPAN, C), 1)

    @pl.loop(0, count)
    def _(span):
        slot = lax.rem(span, 2)
        base = span * SPAN

        @pl.when(span + 1 < count)
        def _():
            fetch(span + 1, 1 - slot).start()

        fetch(span, slot).wait()

        for k in range(SPAN):
            mixed = itab[...] + mix_ref[base + k]
            mixed = mixed ^ shift_right(mixed, 16)
            mixed = mixed * jnp.int32(MUL_MIX)
            mixed = mixed ^ shift_right(mixed, 16)
            mixed = mixed * jnp.int32(MUL_MIX)
            mixed = mixed ^ shift_right(mixed, 16)
            field = shift_right(mixed, 8).astype(F32) * NOISE_A + NOISE_B
            noise[k] = field
            pixels = dot(perm[...], buf[slot, k])
            value = sa_ref[base + k] * pixels + sb_ref[base + k] * field
            noisy[k] = value
            stat[0, pl.ds(k, 1), :] = jnp.sum(value, axis=0, keepdims=True)
            stat[1, pl.ds(k, 1), :] = jnp.sum(value * value, axis=0, keepdims=True)

        rows8 = pl.ds(pl.multiple_of(base, SPAN), SPAN)
        seg = col_ref[0, rows8, :]
        inv_count = col_ref[1, rows8, :]
        first = jnp.zeros((SPAN, C), F32)
        square = jnp.zeros((SPAN, C), F32)
        for k in range(SPAN):
            member = seg == seg_ref[base + k]
            first += jnp.where(member, stat[0, pl.ds(k, 1), :], 0.0)
            square += jnp.where(member, stat[1, pl.ds(k, 1), :], 0.0)
        mean = group_sum(first, lane8) * inv_count
        var = group_sum(square, lane8) * inv_count - mean * mean
        spread = lax.rsqrt(var + 1e-05)
        factor = spread * gain_ref[...] * (1.0 + modul[rows8, :C])
        shift = modul[rows8, C:]
        stat[0] = mean
        stat[1] = factor
        stat[2] = shift
        stat[3] = spread

        for k in range(SPAN):
            one = pl.ds(k, 1)
            centre = noisy[k] - stat[0, one, :]
            normal = (centre * stat[1, one, :] + stat[2, one, :]).astype(BF16)
            x_s[k] = normal
            half = dot(normal, win_h[...])
            th = jnp.tanh(half)
            q = 1.0 + th
            h = half * q
            slope[k] = q + h * (1.0 - th)
            hb = h.astype(BF16)
            hid[k] = hb
            out = dot(hb, wout_ref[...]) + noisy[k]
            resid[k] = out
            outb = out.astype(BF16)
            for j in range(4):
                patch[pl.ds(k * 64, 64), pl.ds(j * C, C)] = outb[j * 64:(j + 1) * 64]

        for m in range(4):
            rows = pl.ds(m * 128, 128)
            half = dot(patch[rows, :], wdown_h[...])
            th = jnp.tanh(half)
            q = 1.0 + th
            h = half * q
            dslope[rows, :] = q + h * (1.0 - th)
            hb = h.astype(BF16)
            dact[rows, :] = hb
            lifted = dot(hb, wup_ref[...])
            for t in range(2):
                k = m * 2 + t
                weight = weight_ref[base + k]
                total = jnp.zeros((64, C), F32)
                for j in range(4):
                    part = pl.ds(j * 64, 64)
                    err = (
                        resid[k, part, :]
                        + lifted[t * 64:(t + 1) * 64, j * C:(j + 1) * C]
                        - noise[k, part, :]
                    )
                    total += err * err
                    gp = err * weight
                    resid[k, part, :] = gp
                    glift[pl.ds(k * 64, 64), pl.ds(j * C, C)] = gp.astype(BF16)
                loss_s[pl.ds(base + k, 1), :] = jnp.sum(total, axis=0, keepdims=True)
            gpd = (dot_bt(glift[rows, :], wup_h[...]) * dslope[rows, :]).astype(BF16)
            gpd_s[rows, :] = gpd
            back = dot_bt(gpd, wdown_ref[...])
            for t in range(2):
                k = m * 2 + t
                for j in range(4):
                    part = pl.ds(j * 64, 64)
                    gres[k, part, :] = (
                        resid[k, part, :] + back[t * 64:(t + 1) * 64, j * C:(j + 1) * C]
                    ).astype(BF16)

        for k in range(SPAN):
            one = pl.ds(k, 1)
            gph = (dot_bt(gres[k], wout_h[...]) * slope[k]).astype(BF16)
            gph_s[k] = gph
            gn = dot_bt(gph, win_ref[...])
            centre = noisy[k] - stat[0, one, :]
            s1_s[pl.ds(base + k, 1), :] = jnp.sum(gn, axis=0, keepdims=True)
            s2_s[pl.ds(base + k, 1), :] = (
                jnp.sum(gn * centre, axis=0, keepdims=True) * stat[3, one, :]
            )

        flat = SPAN * PIX
        gup_ref[...] += dot_at(dact[...], glift[...])
        gdown_ref[...] += dot_at(gpd_s[...], patch[...])
        gout_ref[...] += dot_at(gres[...].reshape(flat, C), hid[...].reshape(flat, HID))
        gin_ref[...] += dot_at(x_s[...].reshape(flat, C), gph_s[...].reshape(flat, HID))

    scale1 = 1.0 + modul[:, :C]
    s2 = s2_s[...]
    misc_ref[...] = jnp.zeros_like(misc_ref)
    misc_ref[pl.ds(0, 1), :] = jnp.sum(s2 * scale1, axis=0, keepdims=True)
    tile_loss = jnp.sum(loss_s[...], axis=1, keepdims=True) * col_ref[2]
    hits = slot_ref[...] == lax.broadcasted_iota(jnp.int32, (C, C), 1)
    misc_ref[pl.ds(1, 1), :] = jnp.sum(jnp.where(hits, tile_loss, 0.0), axis=0, keepdims=True)
    emb = emb_ref[...].astype(F32)
    for ref, part in ((s2 * gain_ref[...], 0), (s1_s[...], 1)):
        gt_ref[:, pl.ds(part * C, C)] = lax.dot_general(
            emb, ref, (((0,), (0,)), ((), ())),
            precision=lax.Precision.HIGHEST, preferred_element_type=F32,
        )


def tile_tables(sizes, dests, times, seeds, group, tile_count):
    clip_count = sizes.shape[0]
    ends = jnp.cumsum(sizes, dtype=jnp.int32)
    tile = jnp.arange(tile_count, dtype=jnp.int32)
    owner = jnp.sum((ends[None, :] <= tile[:, None]).astype(jnp.int32), axis=1)
    onehot = (owner[:, None] == jnp.arange(clip_count, dtype=jnp.int32)[None, :]).astype(jnp.int32)
    columns = jnp.stack([ends - sizes, sizes, dests, times, seeds], axis=0)
    found = jnp.sum(onehot[None] * columns[:, None, :], axis=2)
    usable = owner < clip_count
    within = jnp.where(usable, tile - found[0], 0)
    length = jnp.where(usable, found[1], 1)
    step = found[3].astype(F32)
    alpha_bar = jnp.cos(((step + 1.0) / TSTEPS + 0.008) / 1.008 * (math.pi / 2.0)) ** 2
    mix = within * jnp.int32(wrap32(PIX * C * MUL_POS)) + found[4] * jnp.int32(MUL_SEED) + jnp.int32(ADD_POS)
    inv_len = 1.0 / length.astype(F32)
    weight = jnp.where(usable, inv_len * (2.0 / (PIX * C)), 0.0)
    half = EMB // 2
    freq = jnp.exp(-math.log(10000.0) * jnp.arange(half, dtype=F32) / half)
    angle = step[:, None] * freq[None, :]
    emb = jnp.concatenate([jnp.cos(angle), jnp.sin(angle)], axis=1).astype(BF16)
    slot = jnp.where(usable, found[2] * 4 + group, -1)
    cols = jnp.stack([owner.astype(F32), inv_len / (PIX * 4), weight * 0.5], axis=0)
    cols = jnp.broadcast_to(cols[:, :, None], (3, tile_count, C))
    slots = jnp.broadcast_to(slot[:, None], (tile_count, C))
    count = jnp.sum(sizes) // SPAN
    return (
        count.reshape(1), mix, jnp.sqrt(alpha_bar), jnp.sqrt(1.0 - alpha_bar), weight,
        owner.astype(F32), cols, emb, slots,
    )


def local_grads(clip_tiles, sizes, dests, times, seeds, group, w_time, gain, w_in, w_out, w_down, w_up):
    tile_count = clip_tiles.shape[0]
    count, mix, sa, sb, weight, seg, cols, emb, slots = tile_tables(
        sizes, dests, times, seeds, group, tile_count
    )
    smem = pl.BlockSpec(memory_space=pltpu.SMEM)
    vmem = pl.BlockSpec(memory_space=pltpu.VMEM)
    shapes = [(EMB, 2 * C), (8, C), (C, HID), (C, HID), (256, 512), (256, 512)]
    return pl.pallas_call(
        span_kernel,
        out_shape=[jax.ShapeDtypeStruct(s, F32) for s in shapes],
        in_specs=[smem] * 6 + [pl.BlockSpec(memory_space=pl.ANY)] + [vmem] * 9,
        out_specs=[vmem] * 6,
        scratch_shapes=[
            pltpu.VMEM((2, SPAN, PIX, C), BF16),
            pltpu.SemaphoreType.DMA((2,)),
            pltpu.VMEM((PIX, C), jnp.int32),
            pltpu.VMEM((PIX, PIX), BF16),
            pltpu.VMEM((tile_count, 2 * C), F32),
            pltpu.VMEM((SPAN, PIX, C), F32),
            pltpu.VMEM((SPAN, PIX, C), F32),
            pltpu.VMEM((SPAN, PIX, C), BF16),
            pltpu.VMEM((SPAN, PIX, HID), BF16),
            pltpu.VMEM((SPAN, PIX, HID), F32),
            pltpu.VMEM((SPAN, PIX, C), F32),
            pltpu.VMEM((512, 512), BF16),
            pltpu.VMEM((512, 256), BF16),
            pltpu.VMEM((512, 256), F32),
            pltpu.VMEM((512, 512), BF16),
            pltpu.VMEM((512, 256), BF16),
            pltpu.VMEM((SPAN, PIX, C), BF16),
            pltpu.VMEM((SPAN, PIX, HID), BF16),
            pltpu.VMEM((tile_count, C), F32),
            pltpu.VMEM((tile_count, C), F32),
            pltpu.VMEM((tile_count, C), F32),
            pltpu.VMEM((4, SPAN, C), F32),
            pltpu.VMEM((C, HID), BF16),
            pltpu.VMEM((HID, C), BF16),
            pltpu.VMEM((512, 256), BF16),
            pltpu.VMEM((256, 512), BF16),
        ],
        compiler_params=pltpu.CompilerParams(vmem_limit_bytes=56 * 1024 * 1024),
    )(count, mix, sa, sb, weight, seg, clip_tiles, cols, emb, slots, w_time,
      gain.reshape(1, C), w_in, w_out, w_down, w_up)


def body(clip_tiles, clip_size, clip_dest, timesteps, noise_seeds, w_time, gain, w_in, w_out, w_down, w_up):
    group = lax.axis_index("rep")
    me = lax.axis_index("dp") * lax.axis_size("rep") + group
    parts = local_grads(
        clip_tiles, clip_size[0], clip_dest[0], timesteps[0], noise_seeds[0], group,
        w_time, gain, w_in, w_out, w_down, w_up,
    )
    gt, misc, gin, gout, gdown, gup = lax.psum(tuple(parts), ("dp", "rep"))
    own_loss = lax.dynamic_slice_in_dim(misc[1], me, 1)
    return (gt, misc[0], gin, gout.T, gdown.T, gup, own_loss)


def solution(mesh):
    rows = P(("dp", "rep"), None)
    in_specs = (P(("dp", "rep"), None, None), rows, rows, rows, rows) + (P(),) * 6
    out_specs = (P(),) * 6 + (P(("dp", "rep")),)
    return jax.shard_map(body, mesh=mesh, in_specs=in_specs, out_specs=out_specs, check_vma=False)
```

time: 724 us -> 267 us (0.37)
  waiting for transfers between devices: 310 us -> 84.7 us
  local copies, waits for them, and re-layouts: 140 us -> 13.4 us
  matrix products: 93.7 us -> 0 us
  other arithmetic: 40.5 us -> 3.87 us
  blocking collectives: 103 us -> 129 us
  Pallas kernels: 0 us -> 18 us
  starting transfers between devices: 17.6 us -> 0.04 us
    all_to_all x2 -> x0, waiting for transfers between devices: 225 us -> none  [the longest x1 225 us: body(): lax.all_to_all(outgoing, 'dp', split_axis=0, concat_axis=0, tiled=True)]
    dot_general x57 -> x0, matrix products: 93.7 us -> none  [the longest x4 19.1 us: one_block(): jnp.einsum('rpc,ch->rph', normal_in, w_in, preferred_element_type=jnp.flo...]
    reshape x20 -> x1, local copies, waits for them, and re-layouts: 40.9 us -> 0.75 us  [the longest x16 39.1 us: from_patches(): grid = patch_field.reshape(tile_count, TR // 2, TC // 2, 2, 2, channels)]
    while x264 -> x0, local copies, waits for them, and re-layouts: 26.9 us -> none
    psum x1, blocking collectives: 103 us -> 129 us  [body(): gt, misc, gin, gout, gdown, gup = lax.psum(tuple(parts), ('dp', 'rep'))]
    scatter x3 -> x0, local copies, waits for them, and re-layouts: 24.6 us -> none  [the longest x1 21.7 us: body(): outgoing = jnp.zeros((slot_total,) + clip_tiles.shape[1:], clip_tiles.dty...]
    pallas_call x0 -> x1, Pallas kernels: none -> 18 us  [local_grads(): pl.pallas_call(span_kernel, out_shape=[jax.ShapeDtypeStruct(s, F32) for s...]
    all_to_all x2 -> x0, starting transfers between devices: 17.6 us -> none  [the longest x1 8.96 us: body(): lax.all_to_all(outgoing, 'dp', split_axis=0, concat_axis=0, tiled=True)]
  transfers between devices with their start and end apart: 3 -> 1, of which waited for: 2 -> 1; matrix products, arithmetic and copies ran while one was open for 5% -> 0% of each run, Pallas kernels for 0% -> 0%
where the time goes in v1:
time: 267 us; the launch traced here: 266 us
  blocking collectives  129 us (48%)
  waiting for transfers between devices  84.7 us (32%)
  Pallas kernels  18 us (7%)
  between operations  16.7 us (6%)
  local copies, waits for them, and re-layouts  13.4 us (5%)
  other arithmetic  3.87 us (1%)
    psum x1, blocking collectives, body(): gt, misc, gin, gout, gdown, gup = lax.psum(tuple(parts), ('dp', 'rep'))  129 us
    psum x1, waiting for transfers between devices, body(): gt, misc, gin, gout, gdown, gup = lax.psum(tuple(parts), ('dp', 'rep'))  84.6 us
    pallas_call x1, Pallas kernels, local_grads(): pl.pallas_call(span_kernel, out_shape=[jax.ShapeDtypeStruct(s, F32) for s...  18 us
    unnamed x5, local copies, waits for them, and re-layouts  8.8 us
  transfers between devices with their start and end apart: 1, of which 1 were waited for; matrix products, arithmetic and copies ran while one was open for 0% of the time, Pallas kernels for 0%

profile of v1, /device:TPU:1, one launch (start us, length us, event | category | flops | bytes accessed | tf_op | source)
XLA Modules:
  0.0 266.1 jit_solution(1635475140794226816)
XLA Ops:
  7.2 0.0 all-reduce.3.cloned.1.call-start
  7.2 0.7 copy.24
  8.0 0.1 reduce-window.4
  8.1 0.1 reduce.1
  8.2 0.1 convert_reduce_fusion
  8.3 1.3 bitcast_subtract_fusion
  11.5 0.7 stack.4
  12.3 0.1 multiply_reduce_fusion
  12.4 0.6 subtract_sqrt_fusion
  13.7 0.6 bitcast_select_fusion.2
  14.3 0.6 sqrt.6.sa_ref
  14.8 0.3 fusion
  15.1 0.6 pad_maximum_fusion.emb_ref
  15.8 0.7 broadcast_in_dim.45.slot_ref
  16.5 0.8 broadcast_in_dim.43.col_ref
  17.3 18.0 %shard_map.162 = (f32[256,256]{1,0:T(8,128)}, f32[8,128]{1,0:T(8,128)}, f32[128,256]{1,0:T(8,128)}, f32[128,256]{1,0:T(8,128)}, f32[256,512]{1,0:T(8,128)}, /*index=5*/f32[256,512]{1,0:T(8,128)}) custom-call(s32[1]{0:T(128)} %bitcast.count_ref, s32[128]{0:T(128)} %get-tuple-element.50.mix_ref, f32[128]{0:T(128)} %sqrt.6.sa_ref, ...), custom_call_target="tpu_custom_call" | custom-call | tf_op jit(solution)/shard_map/pallas_call | solution.py:266
  35.2 0.0 all-reduce.3.cloned.1.call-update
  35.3 129.5 %psum.43 = f32[8,128]{1,0:T(8,128)S(1)} all-reduce(f32[8,128]{1,0:T(8,128)} %get-tuple-element.14), channel_id=1, replica_groups=mesh['dp'=32,'rep'=4] {'dp','rep'}, use_global_device_ids=true, to_apply=%region_5.6 | all-reduce | flops 1024 | bytes 8192 | tf_op jit(solution)/shard_map/psum | solution.py:311
  164.7 0.5 fusion.12
  165.2 0.6 constant_dynamic-slice_fusion
  165.8 84.6 %all-reduce.3.cloned.1.call-done = (f32[256,256]{1,0:T(8,128)}, f32[128,256]{1,0:T(8,128)}, f32[256,128]{0,1:T(8,128)}, f32[512,256]{0,1:T(8,128)}, f32[256,512]{1,0:T(8,128)}) async-done(((f32[256,256]{1,0:T(8,128)}, f32[128,256]{1,0:T(8,128)}, f32[256,128]{0,1:T(8,128)}, f32[512,256]{0,1:T(8,128)}, f32[256,512]{1,0:T(8,128)}), (f32[256,256]{1,0:T(8,128)}, f32[128,256]{1,0:T(8,128)}, f32[256,128]{0,1:T(8,128)}, ...) | async-done | bytes 1572880 | tf_op jit(solution)/shard_map/psum | solution.py:311
  250.4 1.7 copy.25
  252.1 2.0 copy.26
  254.1 1.7 copy.32
  255.8 1.6 copy.33
  257.4 1.9 copy.34
  (6 shorter events, 0.0 us)
Async XLA Ops:
  7.2 243.3 %all-reduce.3.cloned.1.call-start = ((), (), s32[]{:S(2)}) async-start(), calls=%async_computation | async-start | bytes 3145728 | tf_op jit(solution)/shard_map/psum | solution.py:311
Sparse Core Ops, SparseCore 0:
  35.4 215.0 all-reduce.2

commit v2 on v1

--- a/solution.py
+++ b/solution.py
@@ -1,3 +1,4 @@
+import functools
 import math
 
 import jax
@@ -25,6 +26,10 @@
 NOISE_B = float(np.float32(ROOT3 * (1.0 / 16777216.0 - 1.0)))
 F32 = jnp.float32
 BF16 = jnp.bfloat16
+ROW_TIME, ROW_IN, ROW_OUT, ROW_DOWN, ROW_UP, ROWS = 0, 512, 768, 1024, 2048, 3072
+PARTS = 3
+HALF = ROWS // 2
+PART = HALF // PARTS
 
 
 def wrap32(value):
@@ -51,13 +56,19 @@
 def group_sum(x, lane):
     pair = x + jnp.where(lane % 2 == 0, pltpu.roll(x, 127, 1), pltpu.roll(x, 1, 1))
     return pair + jnp.where(lane % 4 < 2, pltpu.roll(pair, 126, 1), pltpu.roll(pair, 2, 1))
+
+
+def add_blocks(pack_ref, start, value):
+    height = value.shape[0]
+    for j in range(value.shape[1] // C):
+        pack_ref[pl.ds(start + j * height, height), :] += value[:, j * C:(j + 1) * C]
 
 
 def span_kernel(
     count_ref, mix_ref, sa_ref, sb_ref, weight_ref, seg_ref,
     tiles_hbm, col_ref, emb_ref, slot_ref, wt_ref, gain_ref,
     win_ref, wout_ref, wdown_ref, wup_ref,
-    gt_ref, misc_ref, gin_ref, gout_ref, gdown_ref, gup_ref,
+    pack_ref, misc_ref,
     buf, sem, itab, perm, modul, noise, noisy, x_s, hid, slope, resid, patch,
     dact, dslope, glift, gpd_s, gres, gph_s, s1_s, s2_s, loss_s, stat,
     win_h, wout_h, wdown_h, wup_h,
@@ -88,7 +99,7 @@
     wdown_h[...] = wdown_ref[...] * jnp.asarray(0.5, BF16)
     wout_h[...] = wout_ref[...] * jnp.asarray(0.5, BF16)
     wup_h[...] = wup_ref[...] * jnp.asarray(0.5, BF16)
-    for ref in (gin_ref, gout_ref, gdown_ref, gup_ref, s1_s, s2_s, loss_s):
+    for ref in (pack_ref, s1_s, s2_s, loss_s):
         ref[...] = jnp.zeros_like(ref)
     lane8 = lax.broadcasted_iota(jnp.int32, (SPAN, C), 1)
 
@@ -204,10 +215,14 @@
             )
 
         flat = SPAN * PIX
-        gup_ref[...] += dot_at(dact[...], glift[...])
-        gdown_ref[...] += dot_at(gpd_s[...], patch[...])
-        gout_ref[...] += dot_at(gres[...].reshape(flat, C), hid[...].reshape(flat, HID))
-        gin_ref[...] += dot_at(x_s[...].reshape(flat, C), gph_s[...].reshape(flat, HID))
+        add_blocks(pack_ref, ROW_UP, dot_at(dact[...], glift[...]))
+        add_blocks(pack_ref, ROW_DOWN, dot_at(gpd_s[...], patch[...]))
+        add_blocks(
+            pack_ref, ROW_OUT, dot_at(gres[...].reshape(flat, C), hid[...].reshape(flat, HID))
+        )
+        add_blocks(
+            pack_ref, ROW_IN, dot_at(x_s[...].reshape(flat, C), gph_s[...].reshape(flat, HID))
+        )
 
     scale1 = 1.0 + modul[:, :C]
     s2 = s2_s[...]
@@ -218,7 +233,7 @@
     misc_ref[pl.ds(1, 1), :] = jnp.sum(jnp.where(hits, tile_loss, 0.0), axis=0, keepdims=True)
     emb = emb_ref[...].astype(F32)
     for ref, part in ((s2 * gain_ref[...], 0), (s1_s[...], 1)):
-        gt_ref[:, pl.ds(part * C, C)] = lax.dot_general(
+        pack_ref[pl.ds(ROW_TIME + part * EMB, EMB), :] = lax.dot_general(
             emb, ref, (((0,), (0,)), ((), ())),
             precision=lax.Precision.HIGHEST, preferred_element_type=F32,
         )
@@ -262,12 +277,12 @@
     )
     smem = pl.BlockSpec(memory_space=pltpu.SMEM)
     vmem = pl.BlockSpec(memory_space=pltpu.VMEM)
-    shapes = [(EMB, 2 * C), (8, C), (C, HID), (C, HID), (256, 512), (256, 512)]
+    shapes = [(ROWS, C), (8, C)]
     return pl.pallas_call(
         span_kernel,
         out_shape=[jax.ShapeDtypeStruct(s, F32) for s in shapes],
         in_specs=[smem] * 6 + [pl.BlockSpec(memory_space=pl.ANY)] + [vmem] * 9,
-        out_specs=[vmem] * 6,
+        out_specs=[vmem] * 2,
         scratch_shapes=[
             pltpu.VMEM((2, SPAN, PIX, C), BF16),
             pltpu.SemaphoreType.DMA((2,)),
@@ -301,20 +316,236 @@
       gain.reshape(1, C), w_in, w_out, w_down, w_up)
 
 
-def body(clip_tiles, clip_size, clip_dest, timesteps, noise_seeds, w_time, gain, w_in, w_out, w_down, w_up):
+def reduce_kernel(
+    sizes, x_hbm, misc_ref, res, misc_out,
+    acc, other, r1, r2, r3, m_core, m_axes, local_sem, send_sem, recv_sem,
+):
+    dp, z = lax.axis_index("dp"), lax.axis_index("rep")
+    ny = sizes[1]
+    core = lax.rem(dp, 2)
+    chip = lax.div(dp, 2)
+    coord = (lax.div(chip, ny), lax.rem(chip, ny), z)
+
+    def device(x, y, zz, c):
+        return ((x * ny + y) * 2 + c, zz)
+
+    def peer(axis, r):
+        other_coord = lax.rem(coord[axis] + r, sizes[axis])
+        place = list(coord)
+        place[axis] = other_coord
+        return other_coord, device(*place, core)
+
+    sibling = device(*coord, 1 - core)
+    peers = [(axis, r) for axis in range(3) for r in range(1, sizes[axis])]
+    barrier = pltpu.get_barrier_semaphore()
+    for target in [sibling] + [peer(axis, r)[1] for axis, r in peers]:
+        pl.semaphore_signal(barrier, inc=1, device_id=target, device_id_type=pl.DeviceIdType.MESH)
+
+    mine = core * HALF
+    theirs = (1 - core) * HALF
+    local = []
+    for p in range(PARTS):
+        copy = pltpu.make_async_copy(
+            x_hbm.at[pl.ds(pl.multiple_of(mine + p * PART, 8), PART)],
+            acc.at[pl.ds(p * PART, PART)], local_sem.at[p],
+        )
+        copy.start()
+        local.append(copy)
+    pl.semaphore_wait(barrier, 1 + len(peers))
+
+    started = []
+
+    def send(src, dst, target):
+        index = len(started)
+        copy = pltpu.make_async_remote_copy(
+            src_ref=src, dst_ref=dst, send_sem=send_sem.at[index], recv_sem=recv_sem.at[index],
+            device_id=target, device_id_type=pl.DeviceIdType.MESH,
+        )
+        copy.start()
+        started.append(copy)
+        return copy
+
+    m_core_copy = send(misc_ref, m_core, sibling)
+    first = [
+        send(
+            x_hbm.at[pl.ds(pl.multiple_of(theirs + p * PART, 8), PART)],
+            other.at[pl.ds(p * PART, PART)], sibling,
+        )
+        for p in range(PARTS)
+    ]
+
+    order = [[(p + s) % 3 for s in range(3)] for p in range(PARTS)]
+    lengths = []
+    for p in range(PARTS):
+        length, row = PART, []
+        for s in range(3):
+            length //= sizes[order[p][s]]
+            row.append(length)
+        lengths.append(row)
+    landing = (r1, r2, r3)
+    base = [jnp.int32(p * PART) for p in range(PARTS)]
+    starts = [[None] * 3 for _ in range(PARTS)]
+
+    def scatter(p, s):
+        axis, length = order[p][s], lengths[p][s]
+        copies = []
+        for r in range(1, sizes[axis]):
+            q, target = peer(axis, r)
+            rows = pl.ds(pl.multiple_of(base[p] + q * length, 8), length)
+            copies.append(send(acc.at[rows], landing[s].at[p, r - 1], target))
+        base[p] = base[p] + coord[axis] * length
+        starts[p][s] = base[p]
+        return copies
+
+    flying = [None] * PARTS
+    for p in range(PARTS):
+        local[p].wait()
+        first[p].wait_recv()
+        rows = pl.ds(p * PART, PART)
+        acc[rows, :] = acc[rows, :] + other[rows, :]
+        flying[p] = scatter(p, 0)
+    m_core_copy.wait_recv()
+
+    def misc_stage(axis, value):
+        m_axes[axis, coord[axis]] = value
+        return [
+            send(m_axes.at[axis, coord[axis]], m_axes.at[axis, coord[axis]], peer(axis, r)[1])
+            for r in range(1, sizes[axis])
+        ]
+
+    def misc_total(axis, copies):
+        for copy in copies:
+            copy.wait_recv()
+        total = m_axes[axis, 0]
+        for i in range(1, sizes[axis]):
+            total = total + m_axes[axis, i]
+        return total
+
+    misc_copies = misc_stage(0, misc_ref[...] + m_core[...])
+    for s in range(3):
+        for p in range(PARTS):
+            for copy in flying[p]:
+                copy.wait_recv()
+            rows = pl.ds(pl.multiple_of(base[p], 8), lengths[p][s])
+            total = acc[rows, :]
+            for r in range(sizes[order[p][s]] - 1):
+                total = total + landing[s][p, r]
+            if s < 2:
+                acc[rows, :] = total
+                flying[p] = scatter(p, s + 1)
+            else:
+                final = pl.ds(pl.multiple_of(mine + base[p], 8), lengths[p][s])
+                res[final, :] = total
+                flying[p] = gather(p, 2, sizes, order, lengths, starts, mine, peer, send, res)
+        misc_value = misc_total(s, misc_copies)
+        if s < 2:
+            misc_copies = misc_stage(s + 1, misc_value)
+    misc_out[...] = misc_value
+    for s in (1, 0):
+        for p in range(PARTS):
+            for copy in flying[p]:
+                copy.wait_recv()
+            flying[p] = gather(p, s, sizes, order, lengths, starts, mine, peer, send, res)
+    last = []
+    for p in range(PARTS):
+        for copy in flying[p]:
+            copy.wait_recv()
+        rows = pl.ds(pl.multiple_of(mine + p * PART, 8), PART)
+        last.append(send(res.at[rows], res.at[rows], sibling))
+    for copy in last:
+        copy.wait_recv()
+    for copy in started:
+        copy.wait_send()
+
+
+def gather(p, s, sizes, order, lengths, starts, mine, peer, send, res):
+    axis = order[p][s]
+    rows = pl.ds(pl.multiple_of(mine + starts[p][s], 8), lengths[p][s])
+    return [send(res.at[rows], res.at[rows], peer(axis, r)[1]) for r in range(1, sizes[axis])]
+
+
+def all_reduce(packed, misc, sizes):
+    vmem = pl.BlockSpec(memory_space=pltpu.VMEM)
+    most = max(sizes) - 1
+    per_axis = sum(n - 1 for n in sizes)
+    copies = 1 + PARTS + per_axis * (2 * PARTS + 1) + PARTS
+    shapes = []
+    for s in range(3):
+        longest = 0
+        for p in range(PARTS):
+            length = PART
+            for i in range(s + 1):
+                length //= sizes[(p + i) % 3]
+            longest = max(longest, length)
+        shapes.append(longest)
+    return pl.pallas_call(
+        functools.partial(reduce_kernel, sizes),
+        out_shape=[jax.ShapeDtypeStruct((ROWS, C), F32), jax.ShapeDtypeStruct((8, C), F32)],
+        in_specs=[pl.BlockSpec(memory_space=pl.ANY), vmem],
+        out_specs=[vmem, vmem],
+        scratch_shapes=[
+            pltpu.VMEM((HALF, C), F32),
+            pltpu.VMEM((HALF, C), F32),
+            pltpu.VMEM((PARTS, most, shapes[0], C), F32),
+            pltpu.VMEM((PARTS, most, shapes[1], C), F32),
+            pltpu.VMEM((PARTS, most, shapes[2], C), F32),
+            pltpu.VMEM((8, C), F32),
+            pltpu.VMEM((3, max(sizes), 8, C), F32),
+            pltpu.SemaphoreType.DMA((PARTS,)),
+            pltpu.SemaphoreType.DMA((copies,)),
+            pltpu.SemaphoreType.DMA((copies,)),
+        ],
+        compiler_params=pltpu.CompilerParams(
+            collective_id=0, has_side_effects=True, vmem_limit_bytes=32 * 1024 * 1024
+        ),
+    )(packed, misc)
+
+
+def finish_kernel(packed, misc, gt, gain, gin, gout, gdown, gup, own):
+    def block(start, height, j):
+        return packed[pl.ds(start + j * height, height), :]
+
+    for j in range(2):
+        cols = pl.ds(j * C, C)
+        gt[:, cols] = block(ROW_TIME, EMB, j)
+        gin[:, cols] = block(ROW_IN, C, j)
+        gout[cols, :] = block(ROW_OUT, C, j).T
+    for j in range(4):
+        cols = pl.ds(j * C, C)
+        gdown[cols, :] = block(ROW_DOWN, 256, j).T
+        gup[:, cols] = block(ROW_UP, 256, j)
+    gain[...] = misc[pl.ds(0, 1), :]
+    me = lax.axis_index("dp") * lax.axis_size("rep") + lax.axis_index("rep")
+    lane = lax.broadcasted_iota(jnp.int32, (1, C), 1)
+    own[0] = jnp.sum(jnp.where(lane == me, misc[pl.ds(1, 1), :], 0.0))
+
+
+def finish(packed, misc):
+    vmem = pl.BlockSpec(memory_space=pltpu.VMEM)
+    shapes = [(EMB, 2 * C), (1, C), (C, HID), (HID, C), (512, 256), (256, 512), (1,)]
+    return pl.pallas_call(
+        finish_kernel,
+        out_shape=[jax.ShapeDtypeStruct(s, F32) for s in shapes],
+        in_specs=[vmem, vmem],
+        out_specs=[vmem] * 6 + [pl.BlockSpec(memory_space=pltpu.SMEM)],
+        compiler_params=pltpu.CompilerParams(vmem_limit_bytes=32 * 1024 * 1024),
+    )(packed, misc)
+
+
+def body(sizes, clip_tiles, clip_size, clip_dest, timesteps, noise_seeds, w_time, gain, w_in, w_out, w_down, w_up):
     group = lax.axis_index("rep")
-    me = lax.axis_index("dp") * lax.axis_size("rep") + group
-    parts = local_grads(
+    packed, misc = local_grads(
         clip_tiles, clip_size[0], clip_dest[0], timesteps[0], noise_seeds[0], group,
         w_time, gain, w_in, w_out, w_down, w_up,
     )
-    gt, misc, gin, gout, gdown, gup = lax.psum(tuple(parts), ("dp", "rep"))
-    own_loss = lax.dynamic_slice_in_dim(misc[1], me, 1)
-    return (gt, misc[0], gin, gout.T, gdown.T, gup, own_loss)
+    packed, misc = all_reduce(packed, misc, sizes)
+    gt, ggain, gin, gout, gdown, gup, own = finish(packed, misc)
+    return (gt, ggain.reshape(C), gin, gout, gdown, gup, own)
 
 
 def solution(mesh):
     rows = P(("dp", "rep"), None)
     in_specs = (P(("dp", "rep"), None, None), rows, rows, rows, rows) + (P(),) * 6
     out_specs = (P(),) * 6 + (P(("dp", "rep")),)
-    return jax.shard_map(body, mesh=mesh, in_specs=in_specs, out_specs=out_specs, check_vma=False)
+    sizes = (4, mesh.shape["dp"] // 8, mesh.shape["rep"])
+    return jax.shard_map(functools.partial(body, sizes), mesh=mesh, in_specs=in_specs, out_specs=out_specs, check_vma=False)

time: 267 us -> 131 us (0.49)
  blocking collectives: 129 us -> 0 us
  Pallas kernels: 18 us -> 118 us
  waiting for transfers between devices: 84.7 us -> 0 us
  between operations: 16.7 us -> 3.32 us
  local copies, waits for them, and re-layouts: 13.4 us -> 5.6 us
    psum x1 -> x0, blocking collectives: 129 us -> none  [body(): gt, misc, gin, gout, gdown, gup = lax.psum(tuple(parts), ('dp', 'rep'))]
    pallas_call x0 -> x2, Pallas kernels: none -> 89.6 us  [the longest x1 88.2 us: all_reduce(): pl.pallas_call(functools.partial(reduce_kernel, sizes), out_shape=[jax.Sh...]
    psum x1 -> x0, waiting for transfers between devices: 84.6 us -> none  [body(): gt, misc, gin, gout, gdown, gup = lax.psum(tuple(parts), ('dp', 'rep'))]
    pallas_call x1, Pallas kernels: 18 us -> 28 us  [local_grads(): pl.pallas_call(span_kernel, out_shape=[jax.ShapeDtypeStruct(s, F32) for s...]
    unnamed x5 -> x4, local copies, waits for them, and re-layouts: 8.8 us -> 2.09 us
  transfers between devices with their start and end apart: 1 -> 0, of which waited for: 1 -> 0; matrix products, arithmetic and copies ran while one was open for 0% -> 0% of each run, Pallas kernels for 0% -> 0%
where the time goes in v2:
time: 131 us; the launch traced here: 130 us
  Pallas kernels  118 us (90%)
  local copies, waits for them, and re-layouts  5.6 us (4%)
  other arithmetic  3.83 us (3%)
  between operations  3.32 us (3%)
    pallas_call x1, Pallas kernels, all_reduce(): pl.pallas_call(functools.partial(reduce_kernel, sizes), out_shape=[jax.Sh...  88.2 us
    pallas_call x1, Pallas kernels, local_grads(): pl.pallas_call(span_kernel, out_shape=[jax.ShapeDtypeStruct(s, F32) for s...  28 us

profile of v2, /device:TPU:1, one launch (start us, length us, event | category | flops | bytes accessed | tf_op | source)
XLA Modules:
  0.0 130.3 jit_solution(4840796179374782960)
XLA Ops:
  0.6 0.7 copy.20
  1.4 0.1 reduce-window.4
  1.5 0.1 reduce.1
  1.6 0.1 convert_reduce_fusion
  1.7 1.3 bitcast_subtract_fusion
  5.6 0.7 stack.4
  6.3 0.1 multiply_reduce_fusion
  6.5 0.5 bitcast_select_fusion.2
  7.0 0.6 subtract_sqrt_fusion
  7.6 0.5 sqrt.6.sa_ref
  8.2 0.3 fusion
  8.5 0.6 pad_maximum_fusion.emb_ref
  9.1 0.7 broadcast_in_dim.45.slot_ref
  9.8 0.8 broadcast_in_dim.43.col_ref
  10.6 28.0 %shard_map.162 = (f32[3072,128]{1,0:T(8,128)}, f32[8,128]{1,0:T(8,128)}) custom-call(s32[1]{0:T(128)} %bitcast.count_ref, s32[128]{0:T(128)} %get-tuple-element.34.mix_ref, f32[128]{0:T(128)} %sqrt.6.sa_ref, f32[128]{0:T(128)} %get-tuple-element.31.sb_ref, f32[128]{0:T(128)} %get-tuple-element.35.weight_ref, f32[128]{0:T(128)} %get-tuple-element.39.seg_ref, ...), custom_call_target="tpu_custom_call" | custom-call | tf_op jit(solution)/shard_map/pallas_call | solution.py:281
  38.7 0.0 copy-start
  38.7 1.4 %copy-done = f32[3072,128]{1,0:T(8,128)S(1)} copy-done((f32[3072,128]{1,0:T(8,128)S(1)}, f32[3072,128]{1,0:T(8,128)}, u32[]{:S(2)}) %copy-start) | copy-done | bytes 1572888
  40.1 0.0 copy-start.1
  40.1 0.7 copy-done.1
  40.8 88.2 %shard_map.163 = (f32[3072,128]{1,0:T(8,128)S(1)}, f32[8,128]{1,0:T(8,128)S(1)}) custom-call(f32[3072,128]{1,0:T(8,128)S(1)} %copy-done, f32[8,128]{1,0:T(8,128)S(1)} %copy-done.1), custom_call_target="tpu_custom_call" | custom-call | tf_op jit(solution)/shard_map/pallas_call | solution.py:481
  129.0 1.3 %shard_map.164 = (f32[256,256]{1,0:T(8,128)}, f32[1,128]{1,0:T(1,128)}, f32[128,256]{1,0:T(8,128)}, f32[256,128]{1,0:T(8,128)}, f32[512,256]{1,0:T(8,128)}, /*index=5*/f32[256,512]{1,0:T(8,128)}, f32[1]{0:T(128)}) custom-call(f32[3072,128]{1,0:T(8,128)S(1)} %get-tuple-element.20.packed, f32[8,128]{1,0:T(8,128)S(1)} %get-tuple-element.21.misc), custom_call_target="tpu_custom_call" | custom-call | tf_op jit(solution)/shard_map/pallas_call | solution.py:526
  (6 shorter events, 0.0 us)
Async XLA Ops:
  38.7 1.4 %copy-start = (f32[3072,128]{1,0:T(8,128)S(1)}, f32[3072,128]{1,0:T(8,128)}, u32[]{:S(2)}) copy-start(f32[3072,128]{1,0:T(8,128)} %get-tuple-element.18.x_hbm) | copy-start | bytes 4718596
  40.1 0.7 copy-start.1

commit v3 on v2

--- a/solution.py
+++ b/solution.py
@@ -17,6 +17,8 @@
 PIX = 256
 HID = 256
 SPAN = 8
+RUN = 4
+CLIPS = 64
 MUL_POS = 1103515245
 MUL_SEED = 747796405
 ADD_POS = 1013904223
@@ -24,6 +26,7 @@
 ROOT3 = 1.7320508
 NOISE_A = float(np.float32(2.0 * ROOT3 / 16777216.0))
 NOISE_B = float(np.float32(ROOT3 * (1.0 / 16777216.0 - 1.0)))
+CHUNK, SKEW = 8, 1
 F32 = jnp.float32
 BF16 = jnp.bfloat16
 ROW_TIME, ROW_IN, ROW_OUT, ROW_DOWN, ROW_UP, ROWS = 0, 512, 768, 1024, 2048, 3072
@@ -65,15 +68,18 @@
 
 
 def span_kernel(
-    count_ref, mix_ref, sa_ref, sb_ref, weight_ref, seg_ref,
-    tiles_hbm, col_ref, emb_ref, slot_ref, wt_ref, gain_ref,
+    sizes_ref, seeds_ref, tiles_hbm, sizes_row, dest_row, time_row, freq_ref, wt_ref, gain_ref,
     win_ref, wout_ref, wdown_ref, wup_ref,
     pack_ref, misc_ref,
-    buf, sem, itab, perm, modul, noise, noisy, x_s, hid, slope, resid, patch,
+    buf, sem, itab, perm, emb_s, film_scale, film_shift, sa_s, sb_s, weight_s, inv_s,
+    noise, noisy, x_s, hid, slope, resid, patch,
     dact, dslope, glift, gpd_s, gres, gph_s, s1_s, s2_s, loss_s, stat,
     win_h, wout_h, wdown_h, wup_h,
 ):
-    count = count_ref[0]
+    total = sizes_ref[0, 0]
+    for entry in range(1, CLIPS):
+        total += sizes_ref[0, entry]
+    count = total // SPAN
 
     def fetch(span, slot):
         return pltpu.make_async_copy(
@@ -94,7 +100,27 @@
     pquad, prest = prow // 64, prow % 64
     ppix = (2 * (prest // 16) + pquad // 2) * TC + 2 * (prest % 16) + pquad % 2
     perm[...] = jnp.where(ppix == pcol, 1.0, 0.0).astype(BF16)
-    modul[...] = dot(emb_ref[...], wt_ref[...])
+    eye = lax.broadcasted_iota(jnp.int32, (CLIPS, CLIPS), 0) == lax.broadcasted_iota(
+        jnp.int32, (CLIPS, CLIPS), 1
+    )
+
+    def column(values):
+        picked = jnp.sum(jnp.where(eye, values, 0.0), axis=1, keepdims=True)
+        return jnp.broadcast_to(picked, (CLIPS, C))
+
+    step = time_row[...].astype(F32)
+    alpha_bar = jnp.cos(((step + 1.0) / TSTEPS + 0.008) / 1.008 * (math.pi / 2.0)) ** 2
+    sa_s[...] = column(jnp.sqrt(alpha_bar))
+    sb_s[...] = column(jnp.sqrt(1.0 - alpha_bar))
+    inv_len = 1.0 / column(jnp.maximum(sizes_row[...], 1).astype(F32))
+    inv_s[...] = inv_len * (1.0 / (PIX * 4))
+    weight_s[...] = inv_len * (2.0 / (PIX * C))
+    angle = column(step) * freq_ref[...]
+    emb_s[:, :C] = jnp.cos(angle).astype(BF16)
+    emb_s[:, C:] = jnp.sin(angle).astype(BF16)
+    modulation = dot(emb_s[...], wt_ref[...])
+    film_scale[...] = modulation[:, :C]
+    film_shift[...] = modulation[:, C:]
     win_h[...] = win_ref[...] * jnp.asarray(0.5, BF16)
     wdown_h[...] = wdown_ref[...] * jnp.asarray(0.5, BF16)
     wout_h[...] = wout_ref[...] * jnp.asarray(0.5, BF16)
@@ -103,19 +129,35 @@
         ref[...] = jnp.zeros_like(ref)
     lane8 = lax.broadcasted_iota(jnp.int32, (SPAN, C), 1)
 
-    @pl.loop(0, count)
-    def _(span):
-        slot = lax.rem(span, 2)
-        base = span * SPAN
-
-        @pl.when(span + 1 < count)
-        def _():
-            fetch(span + 1, 1 - slot).start()
-
-        fetch(span, slot).wait()
-
+    def marks(span):
+        one = sizes_ref[0, span * RUN]
+        two = one + sizes_ref[0, span * RUN + 1]
+        return one, two, two + sizes_ref[0, span * RUN + 2]
+
+    def owner_of(tile, bounds):
+        return sum((tile >= bound).astype(jnp.int32) for bound in bounds)
+
+    def make_noisy(span, slot):
+        bounds = marks(span)
+        owners = [owner_of(jnp.int32(k), bounds) for k in range(SPAN)]
         for k in range(SPAN):
-            mixed = itab[...] + mix_ref[base + k]
+            if k % 2 == 0:
+                pair = dot(
+                    perm[...], jnp.concatenate([buf[slot, k], buf[slot, k + 1]], axis=1)
+                )
+            entry = span * RUN + owners[k]
+            row = pl.ds(entry, 1)
+            start = jnp.int32(0)
+            for bound in bounds:
+                start = jnp.where(k >= bound, bound, start)
+            mix = (
+                (k - start) * jnp.int32(wrap32(PIX * C * MUL_POS))
+                + seeds_ref[0, entry] * jnp.int32(MUL_SEED) + jnp.int32(ADD_POS)
+            )
+            stat[4, pl.ds(k, 1), :] = inv_s[row, :]
+            stat[5, pl.ds(k, 1), :] = film_scale[row, :]
+            stat[6, pl.ds(k, 1), :] = film_shift[row, :]
+            mixed = itab[...] + mix
             mixed = mixed ^ shift_right(mixed, 16)
             mixed = mixed * jnp.int32(MUL_MIX)
             mixed = mixed ^ shift_right(mixed, 16)
@@ -123,115 +165,195 @@
             mixed = mixed ^ shift_right(mixed, 16)
             field = shift_right(mixed, 8).astype(F32) * NOISE_A + NOISE_B
             noise[k] = field
-            pixels = dot(perm[...], buf[slot, k])
-            value = sa_ref[base + k] * pixels + sb_ref[base + k] * field
+            pixels = pair[:, (k % 2) * C:(k % 2 + 1) * C]
+            value = sa_s[row, :] * pixels + sb_s[row, :] * field
             noisy[k] = value
             stat[0, pl.ds(k, 1), :] = jnp.sum(value, axis=0, keepdims=True)
             stat[1, pl.ds(k, 1), :] = jnp.sum(value * value, axis=0, keepdims=True)
 
-        rows8 = pl.ds(pl.multiple_of(base, SPAN), SPAN)
-        seg = col_ref[0, rows8, :]
-        inv_count = col_ref[1, rows8, :]
+        tile8 = lax.broadcasted_iota(jnp.int32, (SPAN, C), 0)
+        seg = owner_of(tile8, bounds)
+        inv_count = stat[4]
         first = jnp.zeros((SPAN, C), F32)
         square = jnp.zeros((SPAN, C), F32)
         for k in range(SPAN):
-            member = seg == seg_ref[base + k]
+            member = seg == owners[k]
             first += jnp.where(member, stat[0, pl.ds(k, 1), :], 0.0)
             square += jnp.where(member, stat[1, pl.ds(k, 1), :], 0.0)
         mean = group_sum(first, lane8) * inv_count
         var = group_sum(square, lane8) * inv_count - mean * mean
         spread = lax.rsqrt(var + 1e-05)
-        factor = spread * gain_ref[...] * (1.0 + modul[rows8, :C])
-        shift = modul[rows8, C:]
+        factor = spread * gain_ref[...] * (1.0 + stat[5])
+        shift = stat[6]
         stat[0] = mean
         stat[1] = factor
         stat[2] = shift
         stat[3] = spread
 
-        for k in range(SPAN):
-            one = pl.ds(k, 1)
-            centre = noisy[k] - stat[0, one, :]
-            normal = (centre * stat[1, one, :] + stat[2, one, :]).astype(BF16)
-            x_s[k] = normal
-            half = dot(normal, win_h[...])
-            th = jnp.tanh(half)
-            q = 1.0 + th
-            h = half * q
-            slope[k] = q + h * (1.0 - th)
-            hb = h.astype(BF16)
-            hid[k] = hb
-            out = dot(hb, wout_ref[...]) + noisy[k]
-            resid[k] = out
-            outb = out.astype(BF16)
-            for j in range(4):
-                patch[pl.ds(k * 64, 64), pl.ds(j * C, C)] = outb[j * 64:(j + 1) * 64]
-
-        for m in range(4):
-            rows = pl.ds(m * 128, 128)
-            half = dot(patch[rows, :], wdown_h[...])
-            th = jnp.tanh(half)
-            q = 1.0 + th
-            h = half * q
-            dslope[rows, :] = q + h * (1.0 - th)
-            hb = h.astype(BF16)
-            dact[rows, :] = hb
-            lifted = dot(hb, wup_ref[...])
-            for t in range(2):
-                k = m * 2 + t
-                weight = weight_ref[base + k]
-                total = jnp.zeros((64, C), F32)
-                for j in range(4):
-                    part = pl.ds(j * 64, 64)
-                    err = (
-                        resid[k, part, :]
-                        + lifted[t * 64:(t + 1) * 64, j * C:(j + 1) * C]
-                        - noise[k, part, :]
+    @pl.when(count > 0)
+    def _():
+        @pl.when(count > 1)
+        def _():
+            fetch(1, 1).start()
+
+        fetch(0, 0).wait()
+        make_noisy(0, 0)
+
+    @pl.loop(0, count)
+    def _(span):
+        bounds = marks(span)
+        entries = [span * RUN + owner_of(jnp.int32(k), bounds) for k in range(SPAN)]
+        following = jnp.minimum(span + 1, count - 1)
+        slot = lax.rem(span + 1, 2)
+
+        @pl.when(span + 1 < count)
+        def _():
+            fetch(span + 1, slot).wait()
+
+        @pl.when(span + 2 < count)
+        def _():
+            fetch(span + 2, 1 - slot).start()
+
+        def chunk_steps(k0):
+            tiles = range(k0, k0 + CHUNK)
+            rows = pl.ds(k0 * PIX, CHUNK * PIX)
+            quads = pl.ds(k0 * 64, CHUNK * 64)
+            held = {}
+
+            def normalise():
+                for k in tiles:
+                    one = pl.ds(k, 1)
+                    centre = noisy[k] - stat[0, one, :]
+                    x_s[pl.ds(k * PIX, PIX), :] = (
+                        centre * stat[1, one, :] + stat[2, one, :]
+                    ).astype(BF16)
+
+            def project():
+                held["half"] = dot(x_s[rows, :], win_h[...])
+
+            def activate():
+                half = held["half"]
+                th = jnp.tanh(half)
+                q = 1.0 + th
+                h = half * q
+                slope[rows, :] = q + h * (1.0 - th)
+                hid[rows, :] = h.astype(BF16)
+
+            def project_back():
+                held["out"] = dot(hid[rows, :], wout_ref[...])
+
+            def residual():
+                for k in tiles:
+                    at = (k - k0) * PIX
+                    out = held["out"][at:at + PIX] + noisy[k]
+                    resid[k] = out
+                    outb = out.astype(BF16)
+                    for j in range(4):
+                        patch[pl.ds(k * 64, 64), pl.ds(j * C, C)] = outb[j * 64:(j + 1) * 64]
+
+            def down():
+                held["half"] = dot(patch[quads, :], wdown_h[...])
+
+            def down_activate():
+                half = held["half"]
+                th = jnp.tanh(half)
+                q = 1.0 + th
+                h = half * q
+                dslope[quads, :] = q + h * (1.0 - th)
+                dact[quads, :] = h.astype(BF16)
+
+            def up():
+                held["lifted"] = dot(dact[quads, :], wup_ref[...])
+
+            def error():
+                for k in tiles:
+                    at = (k - k0) * 64
+                    row = pl.ds(entries[k], 1)
+                    weight = weight_s[row, :]
+                    total = jnp.zeros((64, C), F32)
+                    for j in range(4):
+                        part = pl.ds(j * 64, 64)
+                        err = (
+                            resid[k, part, :]
+                            + held["lifted"][at:at + 64, j * C:(j + 1) * C]
+                            - noise[k, part, :]
+                        )
+                        total += err * err
+                        gp = err * weight
+                        resid[k, part, :] = gp
+                        glift[pl.ds(k * 64, 64), pl.ds(j * C, C)] = gp.astype(BF16)
+                    loss_s[row, :] += jnp.sum(total, axis=0, keepdims=True)
+
+            def up_back():
+                held["gda"] = dot_bt(glift[quads, :], wup_h[...])
+
+            def down_slope():
+                gpd_s[quads, :] = (held["gda"] * dslope[quads, :]).astype(BF16)
+
+            def down_back():
+                held["back"] = dot_bt(gpd_s[quads, :], wdown_ref[...])
+
+            def grad_residual():
+                for k in tiles:
+                    at = (k - k0) * 64
+                    for j in range(4):
+                        part = pl.ds(j * 64, 64)
+                        gres[pl.ds(k * PIX + j * 64, 64), :] = (
+                            resid[k, part, :] + held["back"][at:at + 64, j * C:(j + 1) * C]
+                        ).astype(BF16)
+
+            def out_back():
+                held["gh"] = dot_bt(gres[rows, :], wout_h[...])
+
+            def hidden_slope():
+                gph_s[rows, :] = (held["gh"] * slope[rows, :]).astype(BF16)
+
+            def in_back():
+                held["gn"] = dot_bt(gph_s[rows, :], win_ref[...])
+
+            def tile_sums():
+                for k in tiles:
+                    at = (k - k0) * PIX
+                    one = pl.ds(k, 1)
+                    centre = noisy[k] - stat[0, one, :]
+                    mine = held["gn"][at:at + PIX]
+                    row = pl.ds(entries[k], 1)
+                    s1_s[row, :] += jnp.sum(mine, axis=0, keepdims=True)
+                    s2_s[row, :] += (
+                        jnp.sum(mine * centre, axis=0, keepdims=True) * stat[3, one, :]
                     )
-                    total += err * err
-                    gp = err * weight
-                    resid[k, part, :] = gp
-                    glift[pl.ds(k * 64, 64), pl.ds(j * C, C)] = gp.astype(BF16)
-                loss_s[pl.ds(base + k, 1), :] = jnp.sum(total, axis=0, keepdims=True)
-            gpd = (dot_bt(glift[rows, :], wup_h[...]) * dslope[rows, :]).astype(BF16)
-            gpd_s[rows, :] = gpd
-            back = dot_bt(gpd, wdown_ref[...])
-            for t in range(2):
-                k = m * 2 + t
-                for j in range(4):
-                    part = pl.ds(j * 64, 64)
-                    gres[k, part, :] = (
-                        resid[k, part, :] + back[t * 64:(t + 1) * 64, j * C:(j + 1) * C]
-                    ).astype(BF16)
-
-        for k in range(SPAN):
-            one = pl.ds(k, 1)
-            gph = (dot_bt(gres[k], wout_h[...]) * slope[k]).astype(BF16)
-            gph_s[k] = gph
-            gn = dot_bt(gph, win_ref[...])
-            centre = noisy[k] - stat[0, one, :]
-            s1_s[pl.ds(base + k, 1), :] = jnp.sum(gn, axis=0, keepdims=True)
-            s2_s[pl.ds(base + k, 1), :] = (
-                jnp.sum(gn * centre, axis=0, keepdims=True) * stat[3, one, :]
-            )
-
-        flat = SPAN * PIX
+
+            return [
+                normalise, project, activate, project_back, residual, down, down_activate, up,
+                error, up_back, down_slope, down_back, grad_residual, out_back, hidden_slope,
+                in_back, tile_sums,
+            ]
+
+        chunks = [chunk_steps(k0) for k0 in range(0, SPAN, CHUNK)]
+        for turn in range(len(chunks[0]) + SKEW * (len(chunks) - 1)):
+            for index, steps in enumerate(chunks):
+                if 0 <= turn - SKEW * index < len(steps):
+                    steps[turn - SKEW * index]()
+
+        make_noisy(following, slot)
         add_blocks(pack_ref, ROW_UP, dot_at(dact[...], glift[...]))
         add_blocks(pack_ref, ROW_DOWN, dot_at(gpd_s[...], patch[...]))
         add_blocks(
-            pack_ref, ROW_OUT, dot_at(gres[...].reshape(flat, C), hid[...].reshape(flat, HID))
+            pack_ref, ROW_OUT, dot_at(gres[...], hid[...])
         )
         add_blocks(
-            pack_ref, ROW_IN, dot_at(x_s[...].reshape(flat, C), gph_s[...].reshape(flat, HID))
+            pack_ref, ROW_IN, dot_at(x_s[...], gph_s[...])
         )
 
-    scale1 = 1.0 + modul[:, :C]
+    scale1 = 1.0 + film_scale[...]
     s2 = s2_s[...]
     misc_ref[...] = jnp.zeros_like(misc_ref)
     misc_ref[pl.ds(0, 1), :] = jnp.sum(s2 * scale1, axis=0, keepdims=True)
-    tile_loss = jnp.sum(loss_s[...], axis=1, keepdims=True) * col_ref[2]
-    hits = slot_ref[...] == lax.broadcasted_iota(jnp.int32, (C, C), 1)
-    misc_ref[pl.ds(1, 1), :] = jnp.sum(jnp.where(hits, tile_loss, 0.0), axis=0, keepdims=True)
-    emb = emb_ref[...].astype(F32)
+    clip_loss = jnp.sum(loss_s[...], axis=1, keepdims=True) * weight_s[...] * 0.5
+    place = column((dest_row[...] * lax.axis_size("rep") + lax.axis_index("rep")).astype(F32))
+    hits = place == lax.broadcasted_iota(jnp.int32, (CLIPS, C), 1).astype(F32)
+    misc_ref[pl.ds(1, 1), :] = jnp.sum(jnp.where(hits, clip_loss, 0.0), axis=0, keepdims=True)
+    emb = emb_s[...].astype(F32)
     for ref, part in ((s2 * gain_ref[...], 0), (s1_s[...], 1)):
         pack_ref[pl.ds(ROW_TIME + part * EMB, EMB), :] = lax.dot_general(
             emb, ref, (((0,), (0,)), ((), ())),
@@ -239,80 +361,52 @@
         )
 
 
-def tile_tables(sizes, dests, times, seeds, group, tile_count):
-    clip_count = sizes.shape[0]
-    ends = jnp.cumsum(sizes, dtype=jnp.int32)
-    tile = jnp.arange(tile_count, dtype=jnp.int32)
-    owner = jnp.sum((ends[None, :] <= tile[:, None]).astype(jnp.int32), axis=1)
-    onehot = (owner[:, None] == jnp.arange(clip_count, dtype=jnp.int32)[None, :]).astype(jnp.int32)
-    columns = jnp.stack([ends - sizes, sizes, dests, times, seeds], axis=0)
-    found = jnp.sum(onehot[None] * columns[:, None, :], axis=2)
-    usable = owner < clip_count
-    within = jnp.where(usable, tile - found[0], 0)
-    length = jnp.where(usable, found[1], 1)
-    step = found[3].astype(F32)
-    alpha_bar = jnp.cos(((step + 1.0) / TSTEPS + 0.008) / 1.008 * (math.pi / 2.0)) ** 2
-    mix = within * jnp.int32(wrap32(PIX * C * MUL_POS)) + found[4] * jnp.int32(MUL_SEED) + jnp.int32(ADD_POS)
-    inv_len = 1.0 / length.astype(F32)
-    weight = jnp.where(usable, inv_len * (2.0 / (PIX * C)), 0.0)
-    half = EMB // 2
-    freq = jnp.exp(-math.log(10000.0) * jnp.arange(half, dtype=F32) / half)
-    angle = step[:, None] * freq[None, :]
-    emb = jnp.concatenate([jnp.cos(angle), jnp.sin(angle)], axis=1).astype(BF16)
-    slot = jnp.where(usable, found[2] * 4 + group, -1)
-    cols = jnp.stack([owner.astype(F32), inv_len / (PIX * 4), weight * 0.5], axis=0)
-    cols = jnp.broadcast_to(cols[:, :, None], (3, tile_count, C))
-    slots = jnp.broadcast_to(slot[:, None], (tile_count, C))
-    count = jnp.sum(sizes) // SPAN
-    return (
-        count.reshape(1), mix, jnp.sqrt(alpha_bar), jnp.sqrt(1.0 - alpha_bar), weight,
-        owner.astype(F32), cols, emb, slots,
-    )
-
-
-def local_grads(clip_tiles, sizes, dests, times, seeds, group, w_time, gain, w_in, w_out, w_down, w_up):
-    tile_count = clip_tiles.shape[0]
-    count, mix, sa, sb, weight, seg, cols, emb, slots = tile_tables(
-        sizes, dests, times, seeds, group, tile_count
-    )
+def local_grads(clip_tiles, sizes, dests, times, seeds, w_time, gain, w_in, w_out, w_down, w_up):
     smem = pl.BlockSpec(memory_space=pltpu.SMEM)
     vmem = pl.BlockSpec(memory_space=pltpu.VMEM)
-    shapes = [(ROWS, C), (8, C)]
+    half = EMB // 2
+    freq = np.exp(-math.log(10000.0) * np.arange(half) / half).astype(np.float32)
     return pl.pallas_call(
         span_kernel,
-        out_shape=[jax.ShapeDtypeStruct(s, F32) for s in shapes],
-        in_specs=[smem] * 6 + [pl.BlockSpec(memory_space=pl.ANY)] + [vmem] * 9,
+        out_shape=[jax.ShapeDtypeStruct(s, F32) for s in [(ROWS, C), (8, C)]],
+        in_specs=[smem] * 2 + [pl.BlockSpec(memory_space=pl.ANY)] + [vmem] * 10,
         out_specs=[vmem] * 2,
         scratch_shapes=[
             pltpu.VMEM((2, SPAN, PIX, C), BF16),
             pltpu.SemaphoreType.DMA((2,)),
             pltpu.VMEM((PIX, C), jnp.int32),
             pltpu.VMEM((PIX, PIX), BF16),
-            pltpu.VMEM((tile_count, 2 * C), F32),
+            pltpu.VMEM((CLIPS, EMB), BF16),
+            pltpu.VMEM((CLIPS, C), F32),
+            pltpu.VMEM((CLIPS, C), F32),
+            pltpu.VMEM((CLIPS, C), F32),
+            pltpu.VMEM((CLIPS, C), F32),
+            pltpu.VMEM((CLIPS, C), F32),
+            pltpu.VMEM((CLIPS, C), F32),
             pltpu.VMEM((SPAN, PIX, C), F32),
             pltpu.VMEM((SPAN, PIX, C), F32),
-            pltpu.VMEM((SPAN, PIX, C), BF16),
-            pltpu.VMEM((SPAN, PIX, HID), BF16),
-            pltpu.VMEM((SPAN, PIX, HID), F32),
+            pltpu.VMEM((SPAN * PIX, C), BF16),
+            pltpu.VMEM((SPAN * PIX, HID), BF16),
+            pltpu.VMEM((SPAN * PIX, HID), F32),
             pltpu.VMEM((SPAN, PIX, C), F32),
             pltpu.VMEM((512, 512), BF16),
             pltpu.VMEM((512, 256), BF16),
             pltpu.VMEM((512, 256), F32),
             pltpu.VMEM((512, 512), BF16),
             pltpu.VMEM((512, 256), BF16),
-            pltpu.VMEM((SPAN, PIX, C), BF16),
-            pltpu.VMEM((SPAN, PIX, HID), BF16),
-            pltpu.VMEM((tile_count, C), F32),
-            pltpu.VMEM((tile_count, C), F32),
-            pltpu.VMEM((tile_count, C), F32),
-            pltpu.VMEM((4, SPAN, C), F32),
+            pltpu.VMEM((SPAN * PIX, C), BF16),
+            pltpu.VMEM((SPAN * PIX, HID), BF16),
+            pltpu.VMEM((CLIPS, C), F32),
+            pltpu.VMEM((CLIPS, C), F32),
+            pltpu.VMEM((CLIPS, C), F32),
+            pltpu.VMEM((7, SPAN, C), F32),
             pltpu.VMEM((C, HID), BF16),
             pltpu.VMEM((HID, C), BF16),
             pltpu.VMEM((512, 256), BF16),
             pltpu.VMEM((256, 512), BF16),
         ],
         compiler_params=pltpu.CompilerParams(vmem_limit_bytes=56 * 1024 * 1024),
-    )(count, mix, sa, sb, weight, seg, clip_tiles, cols, emb, slots, w_time,
+    )(sizes, seeds, clip_tiles, sizes, dests, times, freq.reshape(1, half), w_time,
       gain.reshape(1, C), w_in, w_out, w_down, w_up)
 
 
@@ -533,9 +627,8 @@
 
 
 def body(sizes, clip_tiles, clip_size, clip_dest, timesteps, noise_seeds, w_time, gain, w_in, w_out, w_down, w_up):
-    group = lax.axis_index("rep")
     packed, misc = local_grads(
-        clip_tiles, clip_size[0], clip_dest[0], timesteps[0], noise_seeds[0], group,
+        clip_tiles, clip_size, clip_dest, timesteps, noise_seeds,
         w_time, gain, w_in, w_out, w_down, w_up,
     )
     packed, misc = all_reduce(packed, misc, sizes)

time: 131 us -> 96.4 us (0.74)
  Pallas kernels: 118 us -> 93.4 us
  other arithmetic: 3.83 us -> 0 us
  local copies, waits for them, and re-layouts: 5.6 us -> 2.09 us
  between operations: 3.32 us -> 0.66 us
    pallas_call x1, Pallas kernels: 88.2 us -> 38.5 us  [all_reduce(): pl.pallas_call(functools.partial(reduce_kernel, sizes), out_shape=[jax.Sh...]
    pallas_call x1, Pallas kernels: 28 us -> 53.5 us  [local_grads(): pl.pallas_call(span_kernel, out_shape=[jax.ShapeDtypeStruct(s, F32) for s...]
    broadcast_in_dim x2 -> x0, local copies, waits for them, and re-layouts: 1.5 us -> none  [the longest x1 0.79 us: tile_tables(): cols = jnp.broadcast_to(cols[:, :, None], (3, tile_count, C))]
where the time goes in v3:
time: 96.4 us; the launch traced here: 96.2 us
  Pallas kernels  93.4 us (97%)
  local copies, waits for them, and re-layouts  2.09 us (2%)
    pallas_call x1, Pallas kernels, local_grads(): pl.pallas_call(span_kernel, out_shape=[jax.ShapeDtypeStruct(s, F32) for s...  53.5 us
    pallas_call x1, Pallas kernels, all_reduce(): pl.pallas_call(functools.partial(reduce_kernel, sizes), out_shape=[jax.Sh...  38.5 us
    unnamed x4, local copies, waits for them, and re-layouts  2.09 us

profile of v3, /device:TPU:1, one launch (start us, length us, event | category | flops | bytes accessed | tf_op | source)
XLA Modules:
  0.0 96.2 jit_solution(14711696766042108828)
XLA Ops:
  0.6 53.5 %shard_map.171 = (f32[3072,128]{1,0:T(8,128)}, f32[8,128]{1,0:T(8,128)}) custom-call(s32[1,64]{1,0:T(1,128)} %sizes_row.1, s32[1,64]{1,0:T(1,128)} %seeds_ref.1, bf16[128,256,128]{2,1,0:T(8,128)(2,1)} %tiles_hbm.1, s32[1,64]{1,0:T(1,128)} %sizes_row.1, s32[1,64]{1,0:T(1,128)} %dest_row.1, s32[1,64]{1,0:T(1,128)} %time_row.1, ...), custom_call_target="tpu_custom_call" | custom-call | tf_op jit(solution)/shard_map/pallas_call | solution.py:369
  54.2 0.0 copy-start
  54.2 1.4 %copy-done = f32[3072,128]{1,0:T(8,128)S(1)} copy-done((f32[3072,128]{1,0:T(8,128)S(1)}, f32[3072,128]{1,0:T(8,128)}, u32[]{:S(2)}) %copy-start) | copy-done | bytes 1572888
  55.6 0.0 copy-start.1
  55.6 0.7 copy-done.1
  56.3 38.5 %shard_map.172 = (f32[3072,128]{1,0:T(8,128)S(1)}, f32[8,128]{1,0:T(8,128)S(1)}) custom-call(f32[3072,128]{1,0:T(8,128)S(1)} %copy-done, f32[8,128]{1,0:T(8,128)S(1)} %copy-done.1), custom_call_target="tpu_custom_call" | custom-call | tf_op jit(solution)/shard_map/pallas_call | solution.py:575
  94.8 1.3 %shard_map.173 = (f32[256,256]{1,0:T(8,128)}, f32[1,128]{1,0:T(1,128)}, f32[128,256]{1,0:T(8,128)}, f32[256,128]{1,0:T(8,128)}, f32[512,256]{1,0:T(8,128)}, /*index=5*/f32[256,512]{1,0:T(8,128)}, f32[1]{0:T(128)}) custom-call(f32[3072,128]{1,0:T(8,128)S(1)} %get-tuple-element.20.packed, f32[8,128]{1,0:T(8,128)S(1)} %get-tuple-element.21.misc), custom_call_target="tpu_custom_call" | custom-call | tf_op jit(solution)/shard_map/pallas_call | solution.py:620
Async XLA Ops:
  54.2 1.4 %copy-start = (f32[3072,128]{1,0:T(8,128)S(1)}, f32[3072,128]{1,0:T(8,128)}, u32[]{:S(2)}) copy-start(f32[3072,128]{1,0:T(8,128)} %get-tuple-element.18.x_hbm) | copy-start | bytes 4718596
  55.6 0.7 copy-start.1

commit v4 on v3

--- a/solution.py
+++ b/solution.py
@@ -405,7 +405,7 @@
             pltpu.VMEM((512, 256), BF16),
             pltpu.VMEM((256, 512), BF16),
         ],
-        compiler_params=pltpu.CompilerParams(vmem_limit_bytes=56 * 1024 * 1024),
+        compiler_params=pltpu.CompilerParams(vmem_limit_bytes=50 * 1024 * 1024),
     )(sizes, seeds, clip_tiles, sizes, dests, times, freq.reshape(1, half), w_time,
       gain.reshape(1, C), w_in, w_out, w_down, w_up)
 
@@ -476,7 +476,7 @@
             length //= sizes[order[p][s]]
             row.append(length)
         lengths.append(row)
-    landing = (r1, r2, r3)
+    landing = (r1, r2)
     base = [jnp.int32(p * PART) for p in range(PARTS)]
     starts = [[None] * 3 for _ in range(PARTS)]
 
@@ -500,23 +500,23 @@
         flying[p] = scatter(p, 0)
     m_core_copy.wait_recv()
 
-    def misc_stage(axis, value):
-        m_axes[axis, coord[axis]] = value
+    def exchange(slots, axis, value):
+        slots[coord[axis]] = value
         return [
-            send(m_axes.at[axis, coord[axis]], m_axes.at[axis, coord[axis]], peer(axis, r)[1])
+            send(slots.at[coord[axis]], slots.at[coord[axis]], peer(axis, r)[1])
             for r in range(1, sizes[axis])
         ]
 
-    def misc_total(axis, copies):
+    def total_of(slots, axis, copies):
         for copy in copies:
             copy.wait_recv()
-        total = m_axes[axis, 0]
+        total = slots[0]
         for i in range(1, sizes[axis]):
-            total = total + m_axes[axis, i]
+            total = total + slots[i]
         return total
 
-    misc_copies = misc_stage(0, misc_ref[...] + m_core[...])
-    for s in range(3):
+    misc_copies = exchange(m_axes.at[0], 0, misc_ref[...] + m_core[...])
+    for s in range(2):
         for p in range(PARTS):
             for copy in flying[p]:
                 copy.wait_recv()
@@ -524,28 +524,37 @@
             total = acc[rows, :]
             for r in range(sizes[order[p][s]] - 1):
                 total = total + landing[s][p, r]
-            if s < 2:
+            if s == 0:
                 acc[rows, :] = total
-                flying[p] = scatter(p, s + 1)
+                flying[p] = scatter(p, 1)
             else:
-                final = pl.ds(pl.multiple_of(mine + base[p], 8), lengths[p][s])
-                res[final, :] = total
-                flying[p] = gather(p, 2, sizes, order, lengths, starts, mine, peer, send, res)
-        misc_value = misc_total(s, misc_copies)
-        if s < 2:
-            misc_copies = misc_stage(s + 1, misc_value)
-    misc_out[...] = misc_value
-    for s in (1, 0):
-        for p in range(PARTS):
-            for copy in flying[p]:
-                copy.wait_recv()
-            flying[p] = gather(p, s, sizes, order, lengths, starts, mine, peer, send, res)
+                flying[p] = exchange(r3.at[p, :, pl.ds(0, lengths[p][1])], order[p][2], total)
+        misc_copies = exchange(
+            m_axes.at[s + 1], s + 1, total_of(m_axes.at[s], s, misc_copies)
+        )
+    for p in range(PARTS):
+        total = total_of(r3.at[p, :, pl.ds(0, lengths[p][1])], order[p][2], flying[p])
+        res[pl.ds(pl.multiple_of(mine + base[p], 8), lengths[p][1]), :] = total
+        flying[p] = gather(p, 1, sizes, order, lengths, starts, mine, peer, send, res)
+    misc_out[...] = total_of(m_axes.at[2], 2, misc_copies)
     last = []
+
+    def forward(p, q):
+        rows = pl.ds(pl.multiple_of(mine + p * PART + q * lengths[p][0], 8), lengths[p][0])
+        last.append(send(res.at[rows], res.at[rows], sibling))
+
     for p in range(PARTS):
         for copy in flying[p]:
             copy.wait_recv()
-        rows = pl.ds(pl.multiple_of(mine + p * PART, 8), PART)
-        last.append(send(res.at[rows], res.at[rows], sibling))
+        flying[p] = gather(p, 0, sizes, order, lengths, starts, mine, peer, send, res)
+        forward(p, coord[order[p][0]])
+    longest = max(sizes)
+    for r in [i for i in range(1, longest) if i != 2] + [2]:
+        for p in range(PARTS):
+            axis = order[p][0]
+            if r < sizes[axis]:
+                flying[p][r - 1].wait_recv()
+                forward(p, lax.rem(coord[axis] + sizes[axis] - r, sizes[axis]))
     for copy in last:
         copy.wait_recv()
     for copy in started:
@@ -562,9 +571,9 @@
     vmem = pl.BlockSpec(memory_space=pltpu.VMEM)
     most = max(sizes) - 1
     per_axis = sum(n - 1 for n in sizes)
-    copies = 1 + PARTS + per_axis * (2 * PARTS + 1) + PARTS
+    copies = 1 + PARTS + per_axis * (5 * PARTS // 3 + 1) + sum(sizes)
     shapes = []
-    for s in range(3):
+    for s in range(2):
         longest = 0
         for p in range(PARTS):
             length = PART
@@ -582,7 +591,7 @@
             pltpu.VMEM((HALF, C), F32),
             pltpu.VMEM((PARTS, most, shapes[0], C), F32),
             pltpu.VMEM((PARTS, most, shapes[1], C), F32),
-            pltpu.VMEM((PARTS, most, shapes[2], C), F32),
+            pltpu.VMEM((PARTS, max(sizes), shapes[1], C), F32),
             pltpu.VMEM((8, C), F32),
             pltpu.VMEM((3, max(sizes), 8, C), F32),
             pltpu.SemaphoreType.DMA((PARTS,)),
@@ -590,7 +599,7 @@
             pltpu.SemaphoreType.DMA((copies,)),
         ],
         compiler_params=pltpu.CompilerParams(
-            collective_id=0, has_side_effects=True, vmem_limit_bytes=32 * 1024 * 1024
+            collective_id=0, has_side_effects=True, vmem_limit_bytes=16 * 1024 * 1024
         ),
     )(packed, misc)
 

time: 96.4 us -> 97.6 us (1.012)
  local copies, waits for them, and re-layouts: 2.09 us -> 8.4 us
  Pallas kernels: 93.4 us -> 88.2 us
    pallas_call x1, Pallas kernels: 53.5 us -> 22.9 us  [local_grads(): pl.pallas_call(span_kernel, out_shape=[jax.ShapeDtypeStruct(s, F32) for s...]
    pallas_call x1, Pallas kernels: 38.5 us -> 63.9 us  [all_reduce(): pl.pallas_call(functools.partial(reduce_kernel, sizes), out_shape=[jax.Sh...]
    unnamed x4 -> x22, local copies, waits for them, and re-layouts: 2.09 us -> 8.4 us
where the time goes in v4:
time: 97.6 us; the launch traced here: 97.3 us
  Pallas kernels  88.2 us (90%)
  local copies, waits for them, and re-layouts  8.4 us (9%)
    pallas_call x1, Pallas kernels, all_reduce(): pl.pallas_call(functools.partial(reduce_kernel, sizes), out_shape=[jax.Sh...  63.9 us
    pallas_call x1, Pallas kernels, local_grads(): pl.pallas_call(span_kernel, out_shape=[jax.ShapeDtypeStruct(s, F32) for s...  22.9 us
    unnamed x22, local copies, waits for them, and re-layouts  8.4 us

profile of v4, /device:TPU:1, one launch (start us, length us, event | category | flops | bytes accessed | tf_op | source)
XLA Modules:
  0.0 97.3 jit_solution(15317491817034885011)
XLA Ops:
  0.6 0.0 copy-start
  0.6 0.9 copy-done
  1.6 0.0 copy-start.1
  1.6 0.9 copy-done.1
  2.5 0.0 copy-start.2
  2.5 0.9 copy-done.2
  3.4 0.0 copy-start.3
  3.4 0.8 copy-done.3
  4.3 0.0 copy-start.4
  4.3 0.8 copy-done.4
  5.1 0.0 copy-start.5
  5.1 0.7 copy-done.5
  5.8 0.0 copy-start.6
  5.8 0.7 copy-done.6
  6.4 0.0 copy-start.7
  6.4 0.7 copy-done.7
  7.1 0.0 copy-start.8
  7.1 0.7 copy-done.8
  7.7 0.0 copy-start.9
  7.7 0.7 copy-done.9
  8.4 0.0 copy-start.10
  8.4 0.7 copy-done.10
  9.1 22.9 %shard_map.171 = (f32[3072,128]{1,0:T(8,128)S(1)}, f32[8,128]{1,0:T(8,128)S(1)}) custom-call(s32[1,64]{1,0:T(1,128)S(1)} %copy-done.5, s32[1,64]{1,0:T(1,128)S(1)} %copy-done.6, bf16[128,256,128]{2,1,0:T(8,128)(2,1)} %tiles_hbm.1, s32[1,64]{1,0:T(1,128)S(1)} %copy-done.5, s32[1,64]{1,0:T(1,128)S(1)} %copy-done.7, s32[1,64]{1,0:T(1,128)S(1)} %copy-done.8, ...), custom_call_target="tpu_custom_call" | custom-call | tf_op jit(solution)/shard_map/pallas_call | solution.py:369
  32.0 63.9 %shard_map.172 = (f32[3072,128]{1,0:T(8,128)S(1)}, f32[8,128]{1,0:T(8,128)S(1)}) custom-call(f32[3072,128]{1,0:T(8,128)S(1)} %get-tuple-element.18.x_hbm, f32[8,128]{1,0:T(8,128)S(1)} %get-tuple-element.19.misc_ref), custom_call_target="tpu_custom_call" | custom-call | tf_op jit(solution)/shard_map/pallas_call | solution.py:584
  95.9 1.3 %shard_map.173 = (f32[256,256]{1,0:T(8,128)}, f32[1,128]{1,0:T(1,128)}, f32[128,256]{1,0:T(8,128)}, f32[256,128]{1,0:T(8,128)}, f32[512,256]{1,0:T(8,128)}, /*index=5*/f32[256,512]{1,0:T(8,128)}, f32[1]{0:T(128)}) custom-call(f32[3072,128]{1,0:T(8,128)S(1)} %get-tuple-element.20.packed, f32[8,128]{1,0:T(8,128)S(1)} %get-tuple-element.21.misc), custom_call_target="tpu_custom_call" | custom-call | tf_op jit(solution)/shard_map/pallas_call | solution.py:629
Async XLA Ops:
  0.6 1.0 copy-start
  1.6 0.9 copy-start.1
  2.5 0.9 copy-start.2
  3.4 0.8 copy-start.3
  4.3 0.8 copy-start.4
  5.1 0.7 copy-start.5
  5.8 0.7 copy-start.6
  6.4 0.7 copy-start.7
  7.1 0.7 copy-start.8
  7.7 0.7 copy-start.9
  8.4 0.7 copy-start.10

commit v5 on v4

--- a/solution.py
+++ b/solution.py
@@ -68,14 +68,28 @@
 
 
 def span_kernel(
-    sizes_ref, seeds_ref, tiles_hbm, sizes_row, dest_row, time_row, freq_ref, wt_ref, gain_ref,
-    win_ref, wout_ref, wdown_ref, wup_ref,
-    pack_ref, misc_ref,
+    tiles_hbm, sizes_hbm, seeds_hbm, dest_hbm, time_hbm, freq_hbm, wt_hbm, gain_hbm,
+    win_hbm, wout_hbm, wdown_hbm, wup_hbm,
+    pack_ref,
+    sizes_ref, seeds_ref, sizes_row, dest_row, time_row, freq_ref, wt_ref, gain_ref,
+    win_ref, wout_ref, wdown_ref, wup_ref, input_sem,
     buf, sem, itab, perm, emb_s, film_scale, film_shift, sa_s, sb_s, weight_s, inv_s,
     noise, noisy, x_s, hid, slope, resid, patch,
     dact, dslope, glift, gpd_s, gres, gph_s, s1_s, s2_s, loss_s, stat,
     win_h, wout_h, wdown_h, wup_h,
 ):
+    inputs = [
+        pltpu.make_async_copy(source, target, input_sem.at[index])
+        for index, (source, target) in enumerate((
+            (sizes_hbm, sizes_ref), (seeds_hbm, seeds_ref), (sizes_hbm, sizes_row),
+            (time_hbm, time_row), (freq_hbm, freq_ref), (wt_hbm, wt_ref), (gain_hbm, gain_ref),
+            (win_hbm, win_ref), (wout_hbm, wout_ref), (wdown_hbm, wdown_ref),
+            (wup_hbm, wup_ref), (dest_hbm, dest_row),
+        ))
+    ]
+    for copy in inputs:
+        copy.start()
+    inputs[0].wait()
     total = sizes_ref[0, 0]
     for entry in range(1, CLIPS):
         total += sizes_ref[0, entry]
@@ -100,6 +114,11 @@
     pquad, prest = prow // 64, prow % 64
     ppix = (2 * (prest // 16) + pquad // 2) * TC + 2 * (prest % 16) + pquad % 2
     perm[...] = jnp.where(ppix == pcol, 1.0, 0.0).astype(BF16)
+    for ref in (pack_ref, s1_s, s2_s, loss_s):
+        ref[...] = jnp.zeros_like(ref)
+    lane8 = lax.broadcasted_iota(jnp.int32, (SPAN, C), 1)
+    for copy in inputs[1:]:
+        copy.wait()
     eye = lax.broadcasted_iota(jnp.int32, (CLIPS, CLIPS), 0) == lax.broadcasted_iota(
         jnp.int32, (CLIPS, CLIPS), 1
     )
@@ -125,9 +144,6 @@
     wdown_h[...] = wdown_ref[...] * jnp.asarray(0.5, BF16)
     wout_h[...] = wout_ref[...] * jnp.asarray(0.5, BF16)
     wup_h[...] = wup_ref[...] * jnp.asarray(0.5, BF16)
-    for ref in (pack_ref, s1_s, s2_s, loss_s):
-        ref[...] = jnp.zeros_like(ref)
-    lane8 = lax.broadcasted_iota(jnp.int32, (SPAN, C), 1)
 
     def marks(span):
         one = sizes_ref[0, span * RUN]
@@ -347,12 +363,11 @@
 
     scale1 = 1.0 + film_scale[...]
     s2 = s2_s[...]
-    misc_ref[...] = jnp.zeros_like(misc_ref)
-    misc_ref[pl.ds(0, 1), :] = jnp.sum(s2 * scale1, axis=0, keepdims=True)
+    pack_ref[pl.ds(ROWS, 1), :] = jnp.sum(s2 * scale1, axis=0, keepdims=True)
     clip_loss = jnp.sum(loss_s[...], axis=1, keepdims=True) * weight_s[...] * 0.5
     place = column((dest_row[...] * lax.axis_size("rep") + lax.axis_index("rep")).astype(F32))
     hits = place == lax.broadcasted_iota(jnp.int32, (CLIPS, C), 1).astype(F32)
-    misc_ref[pl.ds(1, 1), :] = jnp.sum(jnp.where(hits, clip_loss, 0.0), axis=0, keepdims=True)
+    pack_ref[pl.ds(ROWS + 1, 1), :] = jnp.sum(jnp.where(hits, clip_loss, 0.0), axis=0, keepdims=True)
     emb = emb_s[...].astype(F32)
     for ref, part in ((s2 * gain_ref[...], 0), (s1_s[...], 1)):
         pack_ref[pl.ds(ROW_TIME + part * EMB, EMB), :] = lax.dot_general(
@@ -362,16 +377,28 @@
 
 
 def local_grads(clip_tiles, sizes, dests, times, seeds, w_time, gain, w_in, w_out, w_down, w_up):
-    smem = pl.BlockSpec(memory_space=pltpu.SMEM)
     vmem = pl.BlockSpec(memory_space=pltpu.VMEM)
     half = EMB // 2
     freq = np.exp(-math.log(10000.0) * np.arange(half) / half).astype(np.float32)
     return pl.pallas_call(
         span_kernel,
-        out_shape=[jax.ShapeDtypeStruct(s, F32) for s in [(ROWS, C), (8, C)]],
-        in_specs=[smem] * 2 + [pl.BlockSpec(memory_space=pl.ANY)] + [vmem] * 10,
-        out_specs=[vmem] * 2,
+        out_shape=[jax.ShapeDtypeStruct(s, F32) for s in [(ROWS + 8, C)]],
+        in_specs=[pl.BlockSpec(memory_space=pl.ANY)] * 12,
+        out_specs=[vmem],
         scratch_shapes=[
+            pltpu.SMEM((1, CLIPS), jnp.int32),
+            pltpu.SMEM((1, CLIPS), jnp.int32),
+            pltpu.VMEM((1, CLIPS), jnp.int32),
+            pltpu.VMEM((1, CLIPS), jnp.int32),
+            pltpu.VMEM((1, CLIPS), jnp.int32),
+            pltpu.VMEM((1, C), F32),
+            pltpu.VMEM((EMB, 2 * C), BF16),
+            pltpu.VMEM((1, C), F32),
+            pltpu.VMEM((C, HID), BF16),
+            pltpu.VMEM((HID, C), BF16),
+            pltpu.VMEM((512, 256), BF16),
+            pltpu.VMEM((256, 512), BF16),
+            pltpu.SemaphoreType.DMA((12,)),
             pltpu.VMEM((2, SPAN, PIX, C), BF16),
             pltpu.SemaphoreType.DMA((2,)),
             pltpu.VMEM((PIX, C), jnp.int32),
@@ -405,14 +432,14 @@
             pltpu.VMEM((512, 256), BF16),
             pltpu.VMEM((256, 512), BF16),
         ],
-        compiler_params=pltpu.CompilerParams(vmem_limit_bytes=50 * 1024 * 1024),
-    )(sizes, seeds, clip_tiles, sizes, dests, times, freq.reshape(1, half), w_time,
+        compiler_params=pltpu.CompilerParams(vmem_limit_bytes=56 * 1024 * 1024),
+    )(clip_tiles, sizes, seeds, dests, times, freq.reshape(1, half), w_time,
       gain.reshape(1, C), w_in, w_out, w_down, w_up)
 
 
 def reduce_kernel(
-    sizes, x_hbm, misc_ref, res, misc_out,
-    acc, other, r1, r2, r3, m_core, m_axes, local_sem, send_sem, recv_sem,
+    sizes, x_hbm, res,
+    acc, other, r1, r2, r3, m_own, m_core, m_axes, local_sem, send_sem, recv_sem,
 ):
     dp, z = lax.axis_index("dp"), lax.axis_index("rep")
     ny = sizes[1]
@@ -445,6 +472,9 @@
         )
         copy.start()
         local.append(copy)
+    misc_rows = pl.ds(ROWS, 8)
+    m_local = pltpu.make_async_copy(x_hbm.at[misc_rows], m_own, local_sem.at[PARTS])
+    m_local.start()
     pl.semaphore_wait(barrier, 1 + len(peers))
 
     started = []
@@ -459,7 +489,7 @@
         started.append(copy)
         return copy
 
-    m_core_copy = send(misc_ref, m_core, sibling)
+    m_core_copy = send(x_hbm.at[misc_rows], m_core, sibling)
     first = [
         send(
             x_hbm.at[pl.ds(pl.multiple_of(theirs + p * PART, 8), PART)],
@@ -498,6 +528,7 @@
         rows = pl.ds(p * PART, PART)
         acc[rows, :] = acc[rows, :] + other[rows, :]
         flying[p] = scatter(p, 0)
+    m_local.wait()
     m_core_copy.wait_recv()
 
     def exchange(slots, axis, value):
@@ -515,7 +546,7 @@
             total = total + slots[i]
         return total
 
-    misc_copies = exchange(m_axes.at[0], 0, misc_ref[...] + m_core[...])
+    misc_copies = exchange(m_axes.at[0], 0, m_own[...] + m_core[...])
     for s in range(2):
         for p in range(PARTS):
             for copy in flying[p]:
@@ -536,7 +567,7 @@
         total = total_of(r3.at[p, :, pl.ds(0, lengths[p][1])], order[p][2], flying[p])
         res[pl.ds(pl.multiple_of(mine + base[p], 8), lengths[p][1]), :] = total
         flying[p] = gather(p, 1, sizes, order, lengths, starts, mine, peer, send, res)
-    misc_out[...] = total_of(m_axes.at[2], 2, misc_copies)
+    res[misc_rows, :] = total_of(m_axes.at[2], 2, misc_copies)
     last = []
 
     def forward(p, q):
@@ -567,7 +598,7 @@
     return [send(res.at[rows], res.at[rows], peer(axis, r)[1]) for r in range(1, sizes[axis])]
 
 
-def all_reduce(packed, misc, sizes):
+def all_reduce(packed, sizes):
     vmem = pl.BlockSpec(memory_space=pltpu.VMEM)
     most = max(sizes) - 1
     per_axis = sum(n - 1 for n in sizes)
@@ -583,9 +614,9 @@
         shapes.append(longest)
     return pl.pallas_call(
         functools.partial(reduce_kernel, sizes),
-        out_shape=[jax.ShapeDtypeStruct((ROWS, C), F32), jax.ShapeDtypeStruct((8, C), F32)],
-        in_specs=[pl.BlockSpec(memory_space=pl.ANY), vmem],
-        out_specs=[vmem, vmem],
+        out_shape=jax.ShapeDtypeStruct((ROWS + 8, C), F32),
+        in_specs=[pl.BlockSpec(memory_space=pl.ANY)],
+        out_specs=vmem,
         scratch_shapes=[
             pltpu.VMEM((HALF, C), F32),
             pltpu.VMEM((HALF, C), F32),
@@ -593,18 +624,19 @@
             pltpu.VMEM((PARTS, most, shapes[1], C), F32),
             pltpu.VMEM((PARTS, max(sizes), shapes[1], C), F32),
             pltpu.VMEM((8, C), F32),
+            pltpu.VMEM((8, C), F32),
             pltpu.VMEM((3, max(sizes), 8, C), F32),
-            pltpu.SemaphoreType.DMA((PARTS,)),
+            pltpu.SemaphoreType.DMA((PARTS + 1,)),
             pltpu.SemaphoreType.DMA((copies,)),
             pltpu.SemaphoreType.DMA((copies,)),
         ],
         compiler_params=pltpu.CompilerParams(
             collective_id=0, has_side_effects=True, vmem_limit_bytes=16 * 1024 * 1024
         ),
-    )(packed, misc)
-
-
-def finish_kernel(packed, misc, gt, gain, gin, gout, gdown, gup, own):
+    )(packed)
+
+
+def finish_kernel(packed, gt, gain, gin, gout, gdown, gup, own):
     def block(start, height, j):
         return packed[pl.ds(start + j * height, height), :]
 
@@ -617,31 +649,31 @@
         cols = pl.ds(j * C, C)
         gdown[cols, :] = block(ROW_DOWN, 256, j).T
         gup[:, cols] = block(ROW_UP, 256, j)
-    gain[...] = misc[pl.ds(0, 1), :]
+    gain[...] = packed[pl.ds(ROWS, 1), :]
     me = lax.axis_index("dp") * lax.axis_size("rep") + lax.axis_index("rep")
     lane = lax.broadcasted_iota(jnp.int32, (1, C), 1)
-    own[0] = jnp.sum(jnp.where(lane == me, misc[pl.ds(1, 1), :], 0.0))
-
-
-def finish(packed, misc):
+    own[0] = jnp.sum(jnp.where(lane == me, packed[pl.ds(ROWS + 1, 1), :], 0.0))
+
+
+def finish(packed):
     vmem = pl.BlockSpec(memory_space=pltpu.VMEM)
     shapes = [(EMB, 2 * C), (1, C), (C, HID), (HID, C), (512, 256), (256, 512), (1,)]
     return pl.pallas_call(
         finish_kernel,
         out_shape=[jax.ShapeDtypeStruct(s, F32) for s in shapes],
-        in_specs=[vmem, vmem],
+        in_specs=[vmem],
         out_specs=[vmem] * 6 + [pl.BlockSpec(memory_space=pltpu.SMEM)],
         compiler_params=pltpu.CompilerParams(vmem_limit_bytes=32 * 1024 * 1024),
-    )(packed, misc)
+    )(packed)
 
 
 def body(sizes, clip_tiles, clip_size, clip_dest, timesteps, noise_seeds, w_time, gain, w_in, w_out, w_down, w_up):
-    packed, misc = local_grads(
+    packed, = local_grads(
         clip_tiles, clip_size, clip_dest, timesteps, noise_seeds,
         w_time, gain, w_in, w_out, w_down, w_up,
     )
-    packed, misc = all_reduce(packed, misc, sizes)
-    gt, ggain, gin, gout, gdown, gup, own = finish(packed, misc)
+    packed = all_reduce(packed, sizes)
+    gt, ggain, gin, gout, gdown, gup, own = finish(packed)
     return (gt, ggain.reshape(C), gin, gout, gdown, gup, own)
 
 

time: 97.6 us -> 91.5 us (0.938)
  local copies, waits for them, and re-layouts: 8.4 us -> 1.4 us
  Pallas kernels: 88.2 us -> 89.3 us
    unnamed x22 -> x2, local copies, waits for them, and re-layouts: 8.4 us -> 1.4 us
where the time goes in v5:
time: 91.5 us; the launch traced here: 91.4 us
  Pallas kernels  89.3 us (98%)
  local copies, waits for them, and re-layouts  1.4 us (2%)
    pallas_call x1, Pallas kernels, all_reduce(): pl.pallas_call(functools.partial(reduce_kernel, sizes), out_shape=jax.Sha...  64.1 us
    pallas_call x1, Pallas kernels, local_grads(): pl.pallas_call(span_kernel, out_shape=[jax.ShapeDtypeStruct(s, F32) for s...  23.9 us

profile of v5, /device:TPU:1, one launch (start us, length us, event | category | flops | bytes accessed | tf_op | source)
XLA Modules:
  0.0 91.4 jit_solution(12530147137368331531)
XLA Ops:
  0.6 23.9 %shard_map.171.x_hbm = f32[3080,128]{1,0:T(8,128)} custom-call(bf16[128,256,128]{2,1,0:T(8,128)(2,1)} %tiles_hbm.1, s32[1,64]{1,0:T(1,128)} %sizes_hbm.1, s32[1,64]{1,0:T(1,128)} %seeds_hbm.1, s32[1,64]{1,0:T(1,128)} %dest_hbm.1, s32[1,64]{1,0:T(1,128)} %time_hbm.1, f32[1,128]{1,0:T(1,128)} %constant.2.clone.freq_hbm, bf16[256,256]{1,0:T(8,128)(2,1)} %wt_hbm.1, ...), custom_call_target="tpu_custom_call" | custom-call | tf_op jit(solution)/shard_map/pallas_call | solution.py:383
  24.5 0.0 copy-start
  24.5 1.4 %copy-done = f32[3080,128]{1,0:T(8,128)S(1)} copy-done((f32[3080,128]{1,0:T(8,128)S(1)}, f32[3080,128]{1,0:T(8,128)}, u32[]{:S(2)}) %copy-start) | copy-done | bytes 1576984
  25.9 64.1 %shard_map.172.packed = f32[3080,128]{1,0:T(8,128)S(1)} custom-call(f32[3080,128]{1,0:T(8,128)S(1)} %copy-done), custom_call_target="tpu_custom_call" | custom-call | tf_op jit(solution)/shard_map/pallas_call | solution.py:615
  90.0 1.3 %shard_map.173 = (f32[256,256]{1,0:T(8,128)}, f32[1,128]{1,0:T(1,128)}, f32[128,256]{1,0:T(8,128)}, f32[256,128]{1,0:T(8,128)}, f32[512,256]{1,0:T(8,128)}, /*index=5*/f32[256,512]{1,0:T(8,128)}, f32[1]{0:T(128)}) custom-call(f32[3080,128]{1,0:T(8,128)S(1)} %shard_map.172.packed), custom_call_target="tpu_custom_call" | custom-call | tf_op jit(solution)/shard_map/pallas_call | solution.py:661
Async XLA Ops:
  24.5 1.4 %copy-start = (f32[3080,128]{1,0:T(8,128)S(1)}, f32[3080,128]{1,0:T(8,128)}, u32[]{:S(2)}) copy-start(f32[3080,128]{1,0:T(8,128)} %shard_map.171.x_hbm) | copy-start | bytes 4730884

commit v6 on v5

--- a/solution.py
+++ b/solution.py
@@ -26,7 +26,7 @@
 ROOT3 = 1.7320508
 NOISE_A = float(np.float32(2.0 * ROOT3 / 16777216.0))
 NOISE_B = float(np.float32(ROOT3 * (1.0 / 16777216.0 - 1.0)))
-CHUNK, SKEW = 8, 1
+CHUNK, SKEW = 2, 1
 F32 = jnp.float32
 BF16 = jnp.bfloat16
 ROW_TIME, ROW_IN, ROW_OUT, ROW_DOWN, ROW_UP, ROWS = 0, 512, 768, 1024, 2048, 3072

time: 91.5 us -> 91.3 us (level)
    pallas_call x1, Pallas kernels: 64.1 us -> 51.5 us  [all_reduce(): pl.pallas_call(functools.partial(reduce_kernel, sizes), out_shape=jax.Sha...]
    pallas_call x1, Pallas kernels: 23.9 us -> 36.3 us  [local_grads(): pl.pallas_call(span_kernel, out_shape=[jax.ShapeDtypeStruct(s, F32) for s...]
where the time goes in v6:
time: 91.3 us; the launch traced here: 91.1 us
  Pallas kernels  89.1 us (98%)
  local copies, waits for them, and re-layouts  1.4 us (2%)
    pallas_call x1, Pallas kernels, all_reduce(): pl.pallas_call(functools.partial(reduce_kernel, sizes), out_shape=jax.Sha...  51.5 us
    pallas_call x1, Pallas kernels, local_grads(): pl.pallas_call(span_kernel, out_shape=[jax.ShapeDtypeStruct(s, F32) for s...  36.3 us

profile of v6, /device:TPU:1, one launch (start us, length us, event | category | flops | bytes accessed | tf_op | source)
XLA Modules:
  0.0 91.1 jit_solution(8200360468938710484)
XLA Ops:
  0.6 36.3 %shard_map.171.x_hbm = f32[3080,128]{1,0:T(8,128)} custom-call(bf16[128,256,128]{2,1,0:T(8,128)(2,1)} %tiles_hbm.1, s32[1,64]{1,0:T(1,128)} %sizes_hbm.1, s32[1,64]{1,0:T(1,128)} %seeds_hbm.1, s32[1,64]{1,0:T(1,128)} %dest_hbm.1, s32[1,64]{1,0:T(1,128)} %time_hbm.1, f32[1,128]{1,0:T(1,128)} %constant.2.clone.freq_hbm, bf16[256,256]{1,0:T(8,128)(2,1)} %wt_hbm.1, ...), custom_call_target="tpu_custom_call" | custom-call | tf_op jit(solution)/shard_map/pallas_call | solution.py:383
  36.9 0.0 copy-start
  36.9 1.4 %copy-done = f32[3080,128]{1,0:T(8,128)S(1)} copy-done((f32[3080,128]{1,0:T(8,128)S(1)}, f32[3080,128]{1,0:T(8,128)}, u32[]{:S(2)}) %copy-start) | copy-done | bytes 1576984
  38.3 51.5 %shard_map.172.packed = f32[3080,128]{1,0:T(8,128)S(1)} custom-call(f32[3080,128]{1,0:T(8,128)S(1)} %copy-done), custom_call_target="tpu_custom_call" | custom-call | tf_op jit(solution)/shard_map/pallas_call | solution.py:615
  89.8 1.3 %shard_map.173 = (f32[256,256]{1,0:T(8,128)}, f32[1,128]{1,0:T(1,128)}, f32[128,256]{1,0:T(8,128)}, f32[256,128]{1,0:T(8,128)}, f32[512,256]{1,0:T(8,128)}, /*index=5*/f32[256,512]{1,0:T(8,128)}, f32[1]{0:T(128)}) custom-call(f32[3080,128]{1,0:T(8,128)S(1)} %shard_map.172.packed), custom_call_target="tpu_custom_call" | custom-call | tf_op jit(solution)/shard_map/pallas_call | solution.py:661
Async XLA Ops:
  36.9 1.4 %copy-start = (f32[3080,128]{1,0:T(8,128)S(1)}, f32[3080,128]{1,0:T(8,128)}, u32[]{:S(2)}) copy-start(f32[3080,128]{1,0:T(8,128)} %shard_map.171.x_hbm) | copy-start | bytes 4730884

commit v7 on v6

--- a/solution.py
+++ b/solution.py
@@ -490,14 +490,6 @@
         return copy
 
     m_core_copy = send(x_hbm.at[misc_rows], m_core, sibling)
-    first = [
-        send(
-            x_hbm.at[pl.ds(pl.multiple_of(theirs + p * PART, 8), PART)],
-            other.at[pl.ds(p * PART, PART)], sibling,
-        )
-        for p in range(PARTS)
-    ]
-
     order = [[(p + s) % 3 for s in range(3)] for p in range(PARTS)]
     lengths = []
     for p in range(PARTS):
@@ -510,10 +502,29 @@
     base = [jnp.int32(p * PART) for p in range(PARTS)]
     starts = [[None] * 3 for _ in range(PARTS)]
 
+    def turns(axis):
+        return sorted(range(1, sizes[axis]), key=lambda r: -min(r, sizes[axis] - r))
+
+    def piece(p, r):
+        axis, length = order[p][0], lengths[p][0]
+        return p * PART + lax.rem(coord[axis] + r, sizes[axis]) * length, length
+
+    arrivals = []
+    for turn in range(max(sizes)):
+        for p in range(PARTS):
+            steps = turns(order[p][0]) + [0]
+            if turn < len(steps):
+                start, length = piece(p, steps[turn])
+                copy = send(
+                    x_hbm.at[pl.ds(pl.multiple_of(theirs + start, 8), length)],
+                    other.at[pl.ds(pl.multiple_of(start, 8), length)], sibling,
+                )
+                arrivals.append((p, steps[turn], copy))
+
     def scatter(p, s):
         axis, length = order[p][s], lengths[p][s]
         copies = []
-        for r in range(1, sizes[axis]):
+        for r in turns(axis):
             q, target = peer(axis, r)
             rows = pl.ds(pl.multiple_of(base[p] + q * length, 8), length)
             copies.append(send(acc.at[rows], landing[s].at[p, r - 1], target))
@@ -521,13 +532,19 @@
         starts[p][s] = base[p]
         return copies
 
-    flying = [None] * PARTS
+    flying = [[] for _ in range(PARTS)]
+    for copy in local:
+        copy.wait()
+    for p, r, copy in arrivals:
+        copy.wait_recv()
+        start, length = piece(p, r)
+        rows = pl.ds(pl.multiple_of(start, 8), length)
+        acc[rows, :] = acc[rows, :] + other[rows, :]
+        if r:
+            flying[p].append(send(acc.at[rows], r1.at[p, r - 1], peer(order[p][0], r)[1]))
     for p in range(PARTS):
-        local[p].wait()
-        first[p].wait_recv()
-        rows = pl.ds(p * PART, PART)
-        acc[rows, :] = acc[rows, :] + other[rows, :]
-        flying[p] = scatter(p, 0)
+        base[p] = base[p] + coord[order[p][0]] * lengths[p][0]
+        starts[p][0] = base[p]
     m_local.wait()
     m_core_copy.wait_recv()
 
@@ -595,14 +612,16 @@
 def gather(p, s, sizes, order, lengths, starts, mine, peer, send, res):
     axis = order[p][s]
     rows = pl.ds(pl.multiple_of(mine + starts[p][s], 8), lengths[p][s])
-    return [send(res.at[rows], res.at[rows], peer(axis, r)[1]) for r in range(1, sizes[axis])]
+    far_first = sorted(range(1, sizes[axis]), key=lambda r: -min(r, sizes[axis] - r))
+    copies = {r: send(res.at[rows], res.at[rows], peer(axis, r)[1]) for r in far_first}
+    return [copies[r] for r in range(1, sizes[axis])]
 
 
 def all_reduce(packed, sizes):
     vmem = pl.BlockSpec(memory_space=pltpu.VMEM)
     most = max(sizes) - 1
     per_axis = sum(n - 1 for n in sizes)
-    copies = 1 + PARTS + per_axis * (5 * PARTS // 3 + 1) + sum(sizes)
+    copies = 1 + per_axis * 6 + 2 * sum(sizes)
     shapes = []
     for s in range(2):
         longest = 0

time: 91.3 us -> 90.4 us (level)
  Pallas kernels: 89.1 us -> 87.8 us
    pallas_call x1, Pallas kernels: 51.5 us -> 47 us  [all_reduce(): pl.pallas_call(functools.partial(reduce_kernel, sizes), out_shape=jax.Sha...]
    pallas_call x1, Pallas kernels: 36.3 us -> 39.5 us  [local_grads(): pl.pallas_call(span_kernel, out_shape=[jax.ShapeDtypeStruct(s, F32) for s...]
where the time goes in v7:
time: 90.4 us; the launch traced here: 89.9 us
  Pallas kernels  87.8 us (97%)
  local copies, waits for them, and re-layouts  1.4 us (2%)
    pallas_call x1, Pallas kernels, all_reduce(): pl.pallas_call(functools.partial(reduce_kernel, sizes), out_shape=jax.Sha...  47 us
    pallas_call x1, Pallas kernels, local_grads(): pl.pallas_call(span_kernel, out_shape=[jax.ShapeDtypeStruct(s, F32) for s...  39.5 us

profile of v7, /device:TPU:1, one launch (start us, length us, event | category | flops | bytes accessed | tf_op | source)
XLA Modules:
  0.0 89.9 jit_solution(1300483044041168183)
XLA Ops:
  0.6 39.5 %shard_map.171.x_hbm = f32[3080,128]{1,0:T(8,128)} custom-call(bf16[128,256,128]{2,1,0:T(8,128)(2,1)} %tiles_hbm.1, s32[1,64]{1,0:T(1,128)} %sizes_hbm.1, s32[1,64]{1,0:T(1,128)} %seeds_hbm.1, s32[1,64]{1,0:T(1,128)} %dest_hbm.1, s32[1,64]{1,0:T(1,128)} %time_hbm.1, f32[1,128]{1,0:T(1,128)} %constant.2.clone.freq_hbm, bf16[256,256]{1,0:T(8,128)(2,1)} %wt_hbm.1, ...), custom_call_target="tpu_custom_call" | custom-call | tf_op jit(solution)/shard_map/pallas_call | solution.py:383
  40.1 0.0 copy-start
  40.1 1.4 %copy-done = f32[3080,128]{1,0:T(8,128)S(1)} copy-done((f32[3080,128]{1,0:T(8,128)S(1)}, f32[3080,128]{1,0:T(8,128)}, u32[]{:S(2)}) %copy-start) | copy-done | bytes 1576984
  41.5 47.0 %shard_map.172.packed = f32[3080,128]{1,0:T(8,128)S(1)} custom-call(f32[3080,128]{1,0:T(8,128)S(1)} %copy-done), custom_call_target="tpu_custom_call" | custom-call | tf_op jit(solution)/shard_map/pallas_call | solution.py:634
  88.5 1.3 %shard_map.173 = (f32[256,256]{1,0:T(8,128)}, f32[1,128]{1,0:T(1,128)}, f32[128,256]{1,0:T(8,128)}, f32[256,128]{1,0:T(8,128)}, f32[512,256]{1,0:T(8,128)}, /*index=5*/f32[256,512]{1,0:T(8,128)}, f32[1]{0:T(128)}) custom-call(f32[3080,128]{1,0:T(8,128)S(1)} %shard_map.172.packed), custom_call_target="tpu_custom_call" | custom-call | tf_op jit(solution)/shard_map/pallas_call | solution.py:680
Async XLA Ops:
  40.1 1.4 %copy-start = (f32[3080,128]{1,0:T(8,128)S(1)}, f32[3080,128]{1,0:T(8,128)}, u32[]{:S(2)}) copy-start(f32[3080,128]{1,0:T(8,128)} %shard_map.171.x_hbm) | copy-start | bytes 4730884
